TPU v7x, 32 devices: a whole 2x2x4 slice. The times are simulated.
32 devices in a mesh: plane: 4 (over y, core), strip: 8 (over z, x).
Axes of the slice: x: 2, y: 2, z: 4, core: 2. Of those that a mesh axis runs over, the one named last changes fastest.
Arguments:
- u_field: bfloat16 [256, 64, 576], P('plane', 'strip'), may hold values from -6 to 6
- v_field: bfloat16 [256, 64, 576], P('plane', 'strip'), may hold values from -6 to 6
- sigma: float32 [256], P('plane'), may hold values from 1 to 3
- west: int32 [64, 16], P('strip'), may hold values from 0 to 15, each once within a row
- dinv: bfloat16 [64, 16, 1296], P('strip')
- west_coupling: bfloat16 [64, 16, 1296], P('strip'), may hold values from -0.28 to 0.28
- east_coupling: bfloat16 [64, 16, 1296], P('strip'), may hold values from -0.28 to 0.28
Outputs:
- u_out: bfloat16 [256, 64, 576], P('plane', 'strip')
- v_out: bfloat16 [256, 64, 576], P('plane', 'strip')
Inputs may be any that keep to these rules, and one draw needn't show every extreme that they name: Each row of west is a permutation: every element of a column is the west neighbour of exactly one element of the next column.
All inputs are finite; a program needn't handle non-finite values.
Results may differ from a plain program's by a relative error of at most 0.001.
Values may be sent and summed in bfloat16 or wider, within the bound.
A program may use at most 64 MiB of HBM per device.

v0:
```python
import math

import jax
import jax.numpy as jnp
from jax import lax
from jax.sharding import PartitionSpec as P

NODES = 36


def from_behind(block, axis, distance):
    devices = range(lax.axis_size(axis))
    route = [(i - distance, i) for i in devices if i - distance in devices]
    return lax.ppermute(block, axis, route)


def fourier_tables(count):
    coeff_ids = jnp.arange(count, dtype=jnp.int32)
    plane_ids = jnp.arange(count, dtype=jnp.int32)
    wavenumber = (coeff_ids + 1) // 2
    steps_idx = wavenumber[:, None] * plane_ids[None, :] % count
    angles = steps_idx.astype(jnp.float32) * (2.0 * math.pi / count)
    is_sine = (coeff_ids % 2 == 0) & (coeff_ids > 0)
    basis_rows = jnp.where(is_sine[:, None], jnp.sin(angles), jnp.cos(angles))
    edge_rows = (coeff_ids == 0) | (coeff_ids == count - 1)
    scaling = jnp.where(edge_rows, 1.0 / count, 2.0 / count).astype(jnp.float32)
    return (basis_rows * scaling[:, None], basis_rows.T)


def forward_strip(source, gains, inflow, inverse_blocks, west_blocks, onehots):

    def advance(previous, slices):
        source_col, inverse_col, west_col, onehot = slices
        shifted = jnp.einsum("rs,snl->rnl", onehot, previous, precision=lax.Precision.HIGHEST)
        west_term = jnp.einsum(
            "rij,rjl->ril", west_col.astype(jnp.float32), shifted, precision=lax.Precision.HIGHEST
        )
        reduced = source_col - gains * west_term
        solved = jnp.einsum(
            "rij,rjl->ril",
            inverse_col.astype(jnp.float32),
            reduced,
            precision=lax.Precision.HIGHEST,
        )
        return (solved, reduced)

    return lax.scan(advance, inflow, (source, inverse_blocks, west_blocks, onehots))


def backward_strip(reduced_all, gains, inflow, inverse_blocks, east_blocks, onehots):

    def advance(east_term, slices):
        reduced_col, inverse_col, east_col, onehot = slices
        solved = jnp.einsum(
            "rij,rjl->ril",
            inverse_col.astype(jnp.float32),
            reduced_col - gains * east_term,
            precision=lax.Precision.HIGHEST,
        )
        east_part = jnp.einsum(
            "rij,rjl->ril", east_col.astype(jnp.float32), solved, precision=lax.Precision.HIGHEST
        )
        routed = jnp.einsum("rs,ril->sil", onehot, east_part, precision=lax.Precision.HIGHEST)
        return (routed, solved)

    return lax.scan(
        advance, inflow, (reduced_all, inverse_blocks, east_blocks, onehots), reverse=True
    )


def run_chain(direction, block_count, advance, state, outgoing):
    strip_count = lax.axis_size("strip")
    strip_index = lax.axis_index("strip")
    turn_count = strip_count + block_count - 1

    def one_turn(step_turn, carry):
        incoming = from_behind(carry[0], "strip", direction)
        if direction > 0:
            position = step_turn - strip_index
        else:
            position = step_turn - (strip_count - 1 - strip_index)
        active = (position >= 0) & (position < block_count)
        lane_block = jnp.clip(position, 0, block_count - 1)

        def working(current):
            return advance(incoming, lane_block, current)

        def waiting(current):
            return current

        return lax.cond(active, working, waiting, carry)

    return lax.fori_loop(0, turn_count, one_turn, (outgoing, state))


def on_device(u_field, v_field, sigma, west, dinv, west_coupling, east_coupling):
    planes_dev, columns, flat_width = u_field.shape
    planes = planes_dev * lax.axis_size("plane")
    elem_rows = flat_width // NODES
    forward_table, inverse_table = fourier_tables(planes)
    pieces = (
        lax.all_to_all(u_field, "plane", split_axis=1, concat_axis=0, tiled=True),
        lax.all_to_all(v_field, "plane", split_axis=1, concat_axis=0, tiled=True),
    )
    spec_u, spec_v = tuple(
        (
            jnp.einsum(
                "kz,zcn->kcn",
                forward_table,
                piece.astype(jnp.float32),
                precision=lax.Precision.HIGHEST,
            )
            for piece in pieces
        )
    )
    mode_u, mode_v = (
        lax.all_to_all(spec_u, "plane", split_axis=0, concat_axis=1, tiled=True),
        lax.all_to_all(spec_v, "plane", split_axis=0, concat_axis=1, tiled=True),
    )
    modes_dev = mode_u.shape[0]
    lane_count = 2 * modes_dev
    stacked = (
        jnp.concatenate([mode_u, mode_v], 0)
        .reshape(lane_count, columns, elem_rows, NODES)
        .transpose(1, 2, 3, 0)
    )
    lane_gains = jnp.concatenate([sigma, sigma], 0)
    block_count = 1
    lane_width = lane_count // block_count
    onehots = (west[:, :, None] == jnp.arange(elem_rows, dtype=jnp.int32)[None, None, :]).astype(
        jnp.float32
    )
    inverse_blocks = dinv.reshape(columns, elem_rows, NODES, NODES)
    west_blocks = west_coupling.reshape(columns, elem_rows, NODES, NODES)
    east_blocks = east_coupling.reshape(columns, elem_rows, NODES, NODES)
    edge_zeros = jnp.zeros((elem_rows, NODES, lane_width), jnp.float32)

    def forward_advance(incoming, lane_block, carry):
        last_col, reduced = forward_strip(
            stacked, lane_gains, incoming, inverse_blocks, west_blocks, onehots
        )
        return (last_col, reduced)

    reduced_all = run_chain(1, block_count, forward_advance, jnp.zeros_like(stacked), edge_zeros)[1]

    def backward_advance(incoming, lane_block, carry):
        first_term, solved = backward_strip(
            reduced_all, lane_gains, incoming, inverse_blocks, east_blocks, onehots
        )
        return (first_term, solved)

    solved_all = run_chain(-1, block_count, backward_advance, jnp.zeros_like(stacked), edge_zeros)[
        1
    ]
    result_modes = solved_all.transpose(3, 0, 1, 2).reshape(lane_count, columns, flat_width)
    out_modes_u = result_modes[:modes_dev]
    out_modes_v = result_modes[modes_dev:]
    pieces = (
        lax.all_to_all(out_modes_u, "plane", split_axis=1, concat_axis=0, tiled=True),
        lax.all_to_all(out_modes_v, "plane", split_axis=1, concat_axis=0, tiled=True),
    )
    phys_u, phys_v = tuple(
        (
            jnp.einsum("zk,kcn->zcn", inverse_table, piece, precision=lax.Precision.HIGHEST).astype(
                jnp.bfloat16
            )
            for piece in pieces
        )
    )
    u_out, v_out = (
        lax.all_to_all(phys_u, "plane", split_axis=0, concat_axis=1, tiled=True),
        lax.all_to_all(phys_v, "plane", split_axis=0, concat_axis=1, tiled=True),
    )
    return (u_out, v_out)


def solution(mesh):
    in_specs = (
        P("plane", "strip", None),
        P("plane", "strip", None),
        P("plane"),
        P("strip", None),
        P("strip", None, None),
        P("strip", None, None),
        P("strip", None, None),
    )
    out_specs = (P("plane", "strip", None), P("plane", "strip", None))
    return jax.shard_map(
        on_device, mesh=mesh, in_specs=in_specs, out_specs=out_specs, check_vma=False
    )
```

profile of v0, /device:TPU:5, one launch (start us, length us, event | category | flops | bytes accessed | tf_op | source)
XLA Modules:
  0.0 756.9 jit_solution(6093155230600451904)
XLA Ops:
  2.7 3.6 all-to-all-start
  7.2 7.4 all-to-all-done
  14.7 5.3 all-to-all-start.2
  24.1 4.2 all-to-all-done.2
  28.4 5.4 all-to-all-start.1
  37.8 11.3 %all-to-all-done.1 = f32[256,2,576]{2,1,0:T(2,128)S(1)} async-done(((f32[256,2,576]{2,1,0:T(2,128)}), f32[256,2,576]{2,1,0:T(2,128)S(1)}, u32[]{:S(2)}, u32[]{:S(2)}) %all-to-all-start.1) | async-done | bytes 1179680 | tf_op jit(solution)/shard_map/all_to_all | solution.py:117
  49.1 6.2 all-to-all-start.3
  62.8 4.2 copy.113
  67.0 3.7 all-to-all-done.3
  73.1 4.1 copy.119
  84.0 160.6 %while.62 = (s32[]{:T(128)}, f32[16,36,128]{2,1,0:T(8,128)S(1)}, f32[8,16,36,128]{3,2,1,0:T(8,128)}, s32[]{:T(128)}, bf16[8,16,36,36]{3,2,1,0:T(8,128)(2,1)S(1)}...) while((s32[]{:T(128)}, f32[16,36,128]{2,1,0:T(8,128)S(1)}, ...), condition=%wide.region_5.6_spmd.clone, body=%wide.region_0.5_spmd.clone.sunk | while | flops 78008328 | bytes 4606408 | solution.py:93
  84.0 3.8 collective-permute-start.1
  87.9 6.2 collective-permute-done.1
  94.1 23.9 %conditional.6 = ((f32[16,36,128]{2,1,0:T(8,128)S(1)}, f32[8,16,36,128]{3,2,1,0:T(8,128)})) conditional(s32[]{:T(128)} %convert_element_type.80, (f32[16,36,128]{2,1,0:T(8,128)S(1)}, f32[8,16,36,128]{3,2,1,0:T(8,128)}) %tuple.145, (bf16[8,16,36,36]{3,2,1,0:T(8,128)(2,1)S(1)}, f32[8,16,36,128]{3,2,1,0:T(8,128)}, f32[128]{0:T(128)S(1)}, ...), branch_computations={%region_1.1_spmd, %region_2.4_spmd} | conditional | flops 78004224 | bytes 3417805 | solution.py:91
  94.1 23.9 %while.60 = (s32[]{:T(128)}, f32[16,36,128]{2,1,0:T(8,128)S(1)}, f32[8,16,36,128]{3,2,1,0:T(8,128)}, bf16[8,16,36,36]{3,2,1,0:T(8,128)(2,1)S(1)}, f32[8,16,36,12...) while((s32[]{:T(128)}, f32[16,36,128]{2,1,0:T(8,128)S(1)}, ...), condition=%wide.region_4.3_spmd, body=%wide.region_3.2_spmd.sunk | while | flops 78004224 | bytes 2827877 | solution.py:47
  119.5 5.6 collective-permute-done.1
  125.1 28.1 %collective-permute-start.1 = (f32[16,36,128]{2,1,0:T(8,128)S(1)}, f32[16,36,128]{2,1,0:T(8,128)S(1)}, u32[]{:S(2)}, u32[]{:S(2)}) collective-permute-start(f32[16,36,128]{2,1,0:T(8,128)S(1)} %get-tuple-element.1151), channel_id=1, source_target_pairs={{0,1},{1,2},{2,3},{3,4},{4,5},{5,6},{6,7},{8,9},{9,10},{10,11},{11... | collective-permute-start | bytes 884744 | tf_op jit(solution)/shard_map/while/body/eval_jaxpr/ppermute | solution.py:14
  153.3 4.6 collective-permute-done.1
  157.9 4.1 collective-permute-start.1
  162.1 3.9 collective-permute-done.1
  166.0 27.1 %collective-permute-start.1 = (f32[16,36,128]{2,1,0:T(8,128)S(1)}, f32[16,36,128]{2,1,0:T(8,128)S(1)}, u32[]{:S(2)}, u32[]{:S(2)}) collective-permute-start(f32[16,36,128]{2,1,0:T(8,128)S(1)} %get-tuple-element.1151), channel_id=1, source_target_pairs={{0,1},{1,2},{2,3},{3,4},{4,5},{5,6},{6,7},{8,9},{9,10},{10,11},{11... | collective-permute-start | bytes 884744 | tf_op jit(solution)/shard_map/while/body/eval_jaxpr/ppermute | solution.py:14
  193.2 3.9 collective-permute-done.1
  197.1 5.1 collective-permute-start.1
  202.3 3.9 collective-permute-done.1
  206.2 25.3 %collective-permute-start.1 = (f32[16,36,128]{2,1,0:T(8,128)S(1)}, f32[16,36,128]{2,1,0:T(8,128)S(1)}, u32[]{:S(2)}, u32[]{:S(2)}) collective-permute-start(f32[16,36,128]{2,1,0:T(8,128)S(1)} %get-tuple-element.1151), channel_id=1, source_target_pairs={{0,1},{1,2},{2,3},{3,4},{4,5},{5,6},{6,7},{8,9},{9,10},{10,11},{11... | collective-permute-start | bytes 884744 | tf_op jit(solution)/shard_map/while/body/eval_jaxpr/ppermute | solution.py:14
  231.6 3.9 collective-permute-done.1
  235.5 4.7 collective-permute-start.1
  240.3 4.4 collective-permute-done.1
  244.6 3.6 copy.122
  250.0 414.1 %while.63 = (s32[]{:T(128)}, f32[16,36,128]{2,0,1:T(8,128)S(1)}, f32[8,16,36,128]{3,2,1,0:T(8,128)}, s32[]{:T(128)}, bf16[8,16,36,36]{3,2,1,0:T(8,128)(2,1)}, /*...) while((s32[]{:T(128)}, f32[16,36,128]{2,0,1:T(8,128)S(1)}, ...), condition=%wide.region_11.12_spmd.clone, body=%wide.region_6.11_spmd.clone.sunk | while | flops 78008328 | bytes 7490028 | solution.py:93
  251.3 28.2 %collective-permute-done = f32[16,36,128]{2,0,1:T(8,128)S(1)} collective-permute-done((f32[16,36,128]{2,0,1:T(8,128)S(1)}, f32[16,36,128]{2,0,1:T(8,128)S(1)}, u32[]{:S(2)}, u32[]{:S(2)}) %collective-permute-start) | collective-permute-done | bytes 294944 | tf_op jit(solution)/shard_map/while/body/eval_jaxpr/ppermute | solution.py:14
  280.8 9.4 %collective-permute-done = f32[16,36,128]{2,0,1:T(8,128)S(1)} collective-permute-done((f32[16,36,128]{2,0,1:T(8,128)S(1)}, f32[16,36,128]{2,0,1:T(8,128)S(1)}, u32[]{:S(2)}, u32[]{:S(2)}) %collective-permute-start) | collective-permute-done | bytes 294944 | tf_op jit(solution)/shard_map/while/body/eval_jaxpr/ppermute | solution.py:14
  291.5 25.9 %collective-permute-done = f32[16,36,128]{2,0,1:T(8,128)S(1)} collective-permute-done((f32[16,36,128]{2,0,1:T(8,128)S(1)}, f32[16,36,128]{2,0,1:T(8,128)S(1)}, u32[]{:S(2)}, u32[]{:S(2)}) %collective-permute-start) | collective-permute-done | bytes 294944 | tf_op jit(solution)/shard_map/while/body/eval_jaxpr/ppermute | solution.py:14
  318.7 16.6 %collective-permute-done = f32[16,36,128]{2,0,1:T(8,128)S(1)} collective-permute-done((f32[16,36,128]{2,0,1:T(8,128)S(1)}, f32[16,36,128]{2,0,1:T(8,128)S(1)}, u32[]{:S(2)}, u32[]{:S(2)}) %collective-permute-start) | collective-permute-done | bytes 294944 | tf_op jit(solution)/shard_map/while/body/eval_jaxpr/ppermute | solution.py:14
  336.6 19.5 %collective-permute-done = f32[16,36,128]{2,0,1:T(8,128)S(1)} collective-permute-done((f32[16,36,128]{2,0,1:T(8,128)S(1)}, f32[16,36,128]{2,0,1:T(8,128)S(1)}, u32[]{:S(2)}, u32[]{:S(2)}) %collective-permute-start) | collective-permute-done | bytes 294944 | tf_op jit(solution)/shard_map/while/body/eval_jaxpr/ppermute | solution.py:14
  357.5 20.0 %collective-permute-done = f32[16,36,128]{2,0,1:T(8,128)S(1)} collective-permute-done((f32[16,36,128]{2,0,1:T(8,128)S(1)}, f32[16,36,128]{2,0,1:T(8,128)S(1)}, u32[]{:S(2)}, u32[]{:S(2)}) %collective-permute-start) | collective-permute-done | bytes 294944 | tf_op jit(solution)/shard_map/while/body/eval_jaxpr/ppermute | solution.py:14
  378.8 14.7 %collective-permute-done = f32[16,36,128]{2,0,1:T(8,128)S(1)} collective-permute-done((f32[16,36,128]{2,0,1:T(8,128)S(1)}, f32[16,36,128]{2,0,1:T(8,128)S(1)}, u32[]{:S(2)}, u32[]{:S(2)}) %collective-permute-start) | collective-permute-done | bytes 294944 | tf_op jit(solution)/shard_map/while/body/eval_jaxpr/ppermute | solution.py:14
  394.7 236.1 %collective-permute-done = f32[16,36,128]{2,0,1:T(8,128)S(1)} collective-permute-done((f32[16,36,128]{2,0,1:T(8,128)S(1)}, f32[16,36,128]{2,0,1:T(8,128)S(1)}, u32[]{:S(2)}, u32[]{:S(2)}) %collective-permute-start) | collective-permute-done | bytes 294944 | tf_op jit(solution)/shard_map/while/body/eval_jaxpr/ppermute | solution.py:14
  630.9 33.2 %conditional.7 = ((f32[16,36,128]{2,0,1:T(8,128)S(1)}, f32[8,16,36,128]{3,2,1,0:T(8,128)})) conditional(s32[]{:T(128)} %convert_element_type.82, (f32[16,36,128]{2,0,1:T(8,128)S(1)}, f32[8,16,36,128]{3,2,1,0:T(8,128)}) %tuple.148, (f32[8,16,16]{1,2,0:T(8,128)S(1)}, bf16[8,16,36,36]{3,2,1,0:T(8,128)(2,1)}, bf16[8,16,36,36]{3,2,1,0:T(8,128)(2,1)S(1)}, ...), branch_computations={%region_7.7_spmd, %region_8.10_spmd} | conditional | flops 78004224 | bytes 6301425 | solution.py:91
  632.6 31.5 %while.61 = (s32[]{:T(128)}, f32[16,36,128]{2,0,1:T(8,128)S(1)}, f32[8,16,36,128]{3,2,1,0:T(8,128)}, f32[8,16,16]{1,2,0:T(8,128)S(1)}, bf16[8,16,36,36]{3,2,1,0:...) while((s32[]{:T(128)}, f32[16,36,128]{2,0,1:T(8,128)S(1)}, ...), condition=%wide.region_10.9_spmd, body=%wide.region_9.8_spmd.sunk | while | flops 78004224 | bytes 3352189 | solution.py:66
  664.1 3.4 fusion.66
  673.4 18.5 %all-to-all-start.6 = ((f32[64,8,576]{2,0,1:T(8,128)}), f32[64,8,576]{2,0,1:T(8,128)}, u32[]{:S(2)}, u32[]{:S(2)}) async-start(f32[64,8,576]{2,0,1:T(8,128)} %copy.131), calls=%async_computation.6 | async-start | bytes 2621440 | tf_op jit(solution)/shard_map/all_to_all | solution.py:160
  697.9 9.3 %all-to-all-done.6 = f32[64,8,576]{2,0,1:T(8,128)} async-done(((f32[64,8,576]{2,0,1:T(8,128)}), f32[64,8,576]{2,0,1:T(8,128)}, u32[]{:S(2)}, u32[]{:S(2)}) %all-to-all-start.6) | async-done | bytes 1179680 | tf_op jit(solution)/shard_map/all_to_all | solution.py:160
  707.2 5.6 all-to-all-start.4
  719.2 8.9 %all-to-all-done.4 = f32[64,8,576]{2,0,1:T(8,128)S(1)} async-done(((f32[64,8,576]{2,0,1:T(8,128)}), f32[64,8,576]{2,0,1:T(8,128)S(1)}, u32[]{:S(2)}, u32[]{:S(2)}) %all-to-all-start.4) | async-done | bytes 1179680 | tf_op jit(solution)/shard_map/all_to_all | solution.py:159
  728.2 5.4 all-to-all-start.7
  741.9 5.4 all-to-all-start.5
  748.6 7.0 all-to-all-done.5
  (151 shorter events, 127.7 us)
Async XLA Ops:
  0.6 5.7 copy-start.1
  2.7 12.0 %all-to-all-start = ((bf16[64,8,576]{2,0,1:T(8,128)(2,1)}), bf16[64,8,576]{2,0,1:T(8,128)(2,1)S(1)}, u32[]{:S(2)}, u32[]{:S(2)}) async-start(bf16[64,8,576]{2,0,1:T(8,128)(2,1)} %copy.108), calls=%async_computation | async-start | bytes 1310720 | tf_op jit(solution)/shard_map/all_to_all | solution.py:102
  14.7 13.7 %all-to-all-start.2 = ((bf16[64,8,576]{2,0,1:T(8,128)(2,1)}), bf16[64,8,576]{2,0,1:T(8,128)(2,1)S(1)}, u32[]{:S(2)}, u32[]{:S(2)}) async-start(bf16[64,8,576]{2,0,1:T(8,128)(2,1)} %copy.114), calls=%async_computation.2 | async-start | bytes 1310720 | tf_op jit(solution)/shard_map/all_to_all | solution.py:103
  28.4 20.8 %all-to-all-start.1 = ((f32[256,2,576]{2,1,0:T(2,128)}), f32[256,2,576]{2,1,0:T(2,128)S(1)}, u32[]{:S(2)}, u32[]{:S(2)}) async-start(f32[256,2,576]{2,1,0:T(2,128)} %copy.111), calls=%async_computation.1 | async-start | bytes 2621440 | tf_op jit(solution)/shard_map/all_to_all | solution.py:117
  35.7 19.6 %copy-start.3 = (bf16[8,16,1296]{2,1,0:T(8,128)(2,1)S(1)}, bf16[8,16,1296]{2,1,0:T(8,128)(2,1)}, u32[]{:S(2)}) copy-start(bf16[8,16,1296]{2,1,0:T(8,128)(2,1)} %param.23) | copy-start | bytes 995332
  37.8 18.5 %copy-start.4 = (bf16[8,16,1296]{2,1,0:T(8,128)(2,1)S(1)}, bf16[8,16,1296]{2,1,0:T(8,128)(2,1)}, u32[]{:S(2)}) copy-start(bf16[8,16,1296]{2,1,0:T(8,128)(2,1)} %param.24) | copy-start | bytes 995332
  49.1 6.2 copy-start
  49.1 21.5 %all-to-all-start.3 = ((f32[256,2,576]{2,1,0:T(2,128)}), f32[256,2,576]{2,1,0:T(2,128)}, u32[]{:S(2)}, u32[]{:S(2)}) async-start(f32[256,2,576]{2,1,0:T(2,128)} %copy.117), calls=%async_computation.3 | async-start | bytes 2621440 | tf_op jit(solution)/shard_map/all_to_all | solution.py:118
  55.3 4.9 copy-start.5
  82.3 1.7 copy-start.2
  84.0 10.1 %collective-permute-start.1 = (f32[16,36,128]{2,1,0:T(8,128)S(1)}, f32[16,36,128]{2,1,0:T(8,128)S(1)}, u32[]{:S(2)}, u32[]{:S(2)}) collective-permute-start(f32[16,36,128]{2,1,0:T(8,128)S(1)} %get-tuple-element.1151), channel_id=1, source_target_pairs={{0,1},{1,2},{2,3},{3,4},{4,5},{5,6},{6,7},{8,9},{9,10},{10,11},{11... | collective-permute-start | bytes 884744 | tf_op jit(solution)/shard_map/while/body/eval_jaxpr/ppermute | solution.py:14
  118.1 7.0 collective-permute-start.1
  125.1 32.8 %collective-permute-start.1 = (f32[16,36,128]{2,1,0:T(8,128)S(1)}, f32[16,36,128]{2,1,0:T(8,128)S(1)}, u32[]{:S(2)}, u32[]{:S(2)}) collective-permute-start(f32[16,36,128]{2,1,0:T(8,128)S(1)} %get-tuple-element.1151), channel_id=1, source_target_pairs={{0,1},{1,2},{2,3},{3,4},{4,5},{5,6},{6,7},{8,9},{9,10},{10,11},{11... | collective-permute-start | bytes 884744 | tf_op jit(solution)/shard_map/while/body/eval_jaxpr/ppermute | solution.py:14
  157.9 8.1 %collective-permute-start.1 = (f32[16,36,128]{2,1,0:T(8,128)S(1)}, f32[16,36,128]{2,1,0:T(8,128)S(1)}, u32[]{:S(2)}, u32[]{:S(2)}) collective-permute-start(f32[16,36,128]{2,1,0:T(8,128)S(1)} %get-tuple-element.1151), channel_id=1, source_target_pairs={{0,1},{1,2},{2,3},{3,4},{4,5},{5,6},{6,7},{8,9},{9,10},{10,11},{11... | collective-permute-start | bytes 884744 | tf_op jit(solution)/shard_map/while/body/eval_jaxpr/ppermute | solution.py:14
  166.0 31.1 %collective-permute-start.1 = (f32[16,36,128]{2,1,0:T(8,128)S(1)}, f32[16,36,128]{2,1,0:T(8,128)S(1)}, u32[]{:S(2)}, u32[]{:S(2)}) collective-permute-start(f32[16,36,128]{2,1,0:T(8,128)S(1)} %get-tuple-element.1151), channel_id=1, source_target_pairs={{0,1},{1,2},{2,3},{3,4},{4,5},{5,6},{6,7},{8,9},{9,10},{10,11},{11... | collective-permute-start | bytes 884744 | tf_op jit(solution)/shard_map/while/body/eval_jaxpr/ppermute | solution.py:14
  197.1 9.1 %collective-permute-start.1 = (f32[16,36,128]{2,1,0:T(8,128)S(1)}, f32[16,36,128]{2,1,0:T(8,128)S(1)}, u32[]{:S(2)}, u32[]{:S(2)}) collective-permute-start(f32[16,36,128]{2,1,0:T(8,128)S(1)} %get-tuple-element.1151), channel_id=1, source_target_pairs={{0,1},{1,2},{2,3},{3,4},{4,5},{5,6},{6,7},{8,9},{9,10},{10,11},{11... | collective-permute-start | bytes 884744 | tf_op jit(solution)/shard_map/while/body/eval_jaxpr/ppermute | solution.py:14
  206.2 29.3 %collective-permute-start.1 = (f32[16,36,128]{2,1,0:T(8,128)S(1)}, f32[16,36,128]{2,1,0:T(8,128)S(1)}, u32[]{:S(2)}, u32[]{:S(2)}) collective-permute-start(f32[16,36,128]{2,1,0:T(8,128)S(1)} %get-tuple-element.1151), channel_id=1, source_target_pairs={{0,1},{1,2},{2,3},{3,4},{4,5},{5,6},{6,7},{8,9},{9,10},{10,11},{11... | collective-permute-start | bytes 884744 | tf_op jit(solution)/shard_map/while/body/eval_jaxpr/ppermute | solution.py:14
  235.5 9.2 %collective-permute-start.1 = (f32[16,36,128]{2,1,0:T(8,128)S(1)}, f32[16,36,128]{2,1,0:T(8,128)S(1)}, u32[]{:S(2)}, u32[]{:S(2)}) collective-permute-start(f32[16,36,128]{2,1,0:T(8,128)S(1)} %get-tuple-element.1151), channel_id=1, source_target_pairs={{0,1},{1,2},{2,3},{3,4},{4,5},{5,6},{6,7},{8,9},{9,10},{10,11},{11... | collective-permute-start | bytes 884744 | tf_op jit(solution)/shard_map/while/body/eval_jaxpr/ppermute | solution.py:14
  250.0 29.5 %collective-permute-start = (f32[16,36,128]{2,0,1:T(8,128)S(1)}, f32[16,36,128]{2,0,1:T(8,128)S(1)}, u32[]{:S(2)}, u32[]{:S(2)}) collective-permute-start(f32[16,36,128]{2,0,1:T(8,128)S(1)} %get-tuple-element.1184), channel_id=1, source_target_pairs={{1,0},{2,1},{3,2},{4,3},{5,4},{6,5},{7,6},{9,8},{10,9},{11,10},{12... | collective-permute-start | bytes 884744 | tf_op jit(solution)/shard_map/while/body/eval_jaxpr/ppermute | solution.py:14
  279.5 10.7 %collective-permute-start = (f32[16,36,128]{2,0,1:T(8,128)S(1)}, f32[16,36,128]{2,0,1:T(8,128)S(1)}, u32[]{:S(2)}, u32[]{:S(2)}) collective-permute-start(f32[16,36,128]{2,0,1:T(8,128)S(1)} %get-tuple-element.1184), channel_id=1, source_target_pairs={{1,0},{2,1},{3,2},{4,3},{5,4},{6,5},{7,6},{9,8},{10,9},{11,10},{12... | collective-permute-start | bytes 884744 | tf_op jit(solution)/shard_map/while/body/eval_jaxpr/ppermute | solution.py:14
  290.2 27.2 %collective-permute-start = (f32[16,36,128]{2,0,1:T(8,128)S(1)}, f32[16,36,128]{2,0,1:T(8,128)S(1)}, u32[]{:S(2)}, u32[]{:S(2)}) collective-permute-start(f32[16,36,128]{2,0,1:T(8,128)S(1)} %get-tuple-element.1184), channel_id=1, source_target_pairs={{1,0},{2,1},{3,2},{4,3},{5,4},{6,5},{7,6},{9,8},{10,9},{11,10},{12... | collective-permute-start | bytes 884744 | tf_op jit(solution)/shard_map/while/body/eval_jaxpr/ppermute | solution.py:14
  317.4 17.9 %collective-permute-start = (f32[16,36,128]{2,0,1:T(8,128)S(1)}, f32[16,36,128]{2,0,1:T(8,128)S(1)}, u32[]{:S(2)}, u32[]{:S(2)}) collective-permute-start(f32[16,36,128]{2,0,1:T(8,128)S(1)} %get-tuple-element.1184), channel_id=1, source_target_pairs={{1,0},{2,1},{3,2},{4,3},{5,4},{6,5},{7,6},{9,8},{10,9},{11,10},{12... | collective-permute-start | bytes 884744 | tf_op jit(solution)/shard_map/while/body/eval_jaxpr/ppermute | solution.py:14
  335.3 20.9 %collective-permute-start = (f32[16,36,128]{2,0,1:T(8,128)S(1)}, f32[16,36,128]{2,0,1:T(8,128)S(1)}, u32[]{:S(2)}, u32[]{:S(2)}) collective-permute-start(f32[16,36,128]{2,0,1:T(8,128)S(1)} %get-tuple-element.1184), channel_id=1, source_target_pairs={{1,0},{2,1},{3,2},{4,3},{5,4},{6,5},{7,6},{9,8},{10,9},{11,10},{12... | collective-permute-start | bytes 884744 | tf_op jit(solution)/shard_map/while/body/eval_jaxpr/ppermute | solution.py:14
  356.2 21.3 %collective-permute-start = (f32[16,36,128]{2,0,1:T(8,128)S(1)}, f32[16,36,128]{2,0,1:T(8,128)S(1)}, u32[]{:S(2)}, u32[]{:S(2)}) collective-permute-start(f32[16,36,128]{2,0,1:T(8,128)S(1)} %get-tuple-element.1184), channel_id=1, source_target_pairs={{1,0},{2,1},{3,2},{4,3},{5,4},{6,5},{7,6},{9,8},{10,9},{11,10},{12... | collective-permute-start | bytes 884744 | tf_op jit(solution)/shard_map/while/body/eval_jaxpr/ppermute | solution.py:14
  377.5 16.0 %collective-permute-start = (f32[16,36,128]{2,0,1:T(8,128)S(1)}, f32[16,36,128]{2,0,1:T(8,128)S(1)}, u32[]{:S(2)}, u32[]{:S(2)}) collective-permute-start(f32[16,36,128]{2,0,1:T(8,128)S(1)} %get-tuple-element.1184), channel_id=1, source_target_pairs={{1,0},{2,1},{3,2},{4,3},{5,4},{6,5},{7,6},{9,8},{10,9},{11,10},{12... | collective-permute-start | bytes 884744 | tf_op jit(solution)/shard_map/while/body/eval_jaxpr/ppermute | solution.py:14
  393.4 237.4 %collective-permute-start = (f32[16,36,128]{2,0,1:T(8,128)S(1)}, f32[16,36,128]{2,0,1:T(8,128)S(1)}, u32[]{:S(2)}, u32[]{:S(2)}) collective-permute-start(f32[16,36,128]{2,0,1:T(8,128)S(1)} %get-tuple-element.1184), channel_id=1, source_target_pairs={{1,0},{2,1},{3,2},{4,3},{5,4},{6,5},{7,6},{9,8},{10,9},{11,10},{12... | collective-permute-start | bytes 884744 | tf_op jit(solution)/shard_map/while/body/eval_jaxpr/ppermute | solution.py:14
  673.4 33.8 %all-to-all-start.6 = ((f32[64,8,576]{2,0,1:T(8,128)}), f32[64,8,576]{2,0,1:T(8,128)}, u32[]{:S(2)}, u32[]{:S(2)}) async-start(f32[64,8,576]{2,0,1:T(8,128)} %copy.131), calls=%async_computation.6 | async-start | bytes 2621440 | tf_op jit(solution)/shard_map/all_to_all | solution.py:160
  707.2 20.9 %all-to-all-start.4 = ((f32[64,8,576]{2,0,1:T(8,128)}), f32[64,8,576]{2,0,1:T(8,128)S(1)}, u32[]{:S(2)}, u32[]{:S(2)}) async-start(f32[64,8,576]{2,0,1:T(8,128)} %copy.124), calls=%async_computation.4 | async-start | bytes 2621440 | tf_op jit(solution)/shard_map/all_to_all | solution.py:159
  728.2 13.7 %all-to-all-start.7 = ((bf16[256,2,576]{2,1,0:T(2,128)(2,1)}), bf16[256,2,576]{2,1,0:T(2,128)(2,1)S(1)}, u32[]{:S(2)}, u32[]{:S(2)}) async-start(bf16[256,2,576]{2,1,0:T(2,128)(2,1)} %copy.134), calls=%async_computation.7 | async-start | bytes 1310720 | tf_op jit(solution)/shard_map/all_to_all | solution.py:172
  741.9 13.7 %all-to-all-start.5 = ((bf16[256,2,576]{2,1,0:T(2,128)(2,1)}), bf16[256,2,576]{2,1,0:T(2,128)(2,1)S(1)}, u32[]{:S(2)}, u32[]{:S(2)}) async-start(bf16[256,2,576]{2,1,0:T(2,128)(2,1)} %copy.127), calls=%async_computation.5 | async-start | bytes 1310720 | tf_op jit(solution)/shard_map/all_to_all | solution.py:171
where the time goes:
time: 762 us; the launch traced here: 757 us
  waiting for transfers between devices  462 us (61%)
  starting transfers between devices  165 us (22%)
  local copies, waits for them, and re-layouts  59.3 us (8%)
  matrix products  57.1 us (7%)
  other arithmetic  11.9 us (2%)
    ppermute x16, waiting for transfers between devices, from_behind(): return lax.ppermute(block, axis, route)  407 us
    ppermute x16, starting transfers between devices, from_behind(): return lax.ppermute(block, axis, route)  110 us
    all_to_all x1, starting transfers between devices, on_device(): lax.all_to_all(out_modes_v, 'plane', split_axis=1, concat_axis=0, tiled=T...  18.5 us
    dot_general x8, matrix products, advance(): jnp.einsum('rij,rjl->ril', west_col.astype(jnp.float32), shifted, precisi...  17.3 us
  transfers between devices with their start and end apart: 24, of which 24 were waited for; matrix products, arithmetic and copies ran while one was open for 5% of the time, Pallas kernels for 0%

commit v1 on v0

--- a/solution.py
+++ b/solution.py
@@ -2,7 +2,11 @@
 
 import jax
 import jax.numpy as jnp
+import ml_dtypes
+import numpy as np
 from jax import lax
+from jax.experimental import pallas as pl
+from jax.experimental.pallas import tpu as pltpu
 from jax.sharding import PartitionSpec as P
 
 NODES = 36
@@ -93,7 +97,7 @@
     return lax.fori_loop(0, turn_count, one_turn, (outgoing, state))
 
 
-def on_device(u_field, v_field, sigma, west, dinv, west_coupling, east_coupling):
+def strip_chain_on_device(u_field, v_field, sigma, west, dinv, west_coupling, east_coupling):
     planes_dev, columns, flat_width = u_field.shape
     planes = planes_dev * lax.axis_size("plane")
     elem_rows = flat_width // NODES
@@ -174,6 +178,205 @@
     return (u_out, v_out)
 
 
+PAD = 48
+
+
+def split_table(table):
+    high = table.astype(np.float32).astype(ml_dtypes.bfloat16)
+    low = (table - high.astype(np.float64)).astype(ml_dtypes.bfloat16)
+    return jnp.asarray(high), jnp.asarray(low)
+
+
+def transform_tables(count, shares):
+    ids = np.arange(count)
+    angles = 2.0 * np.pi * (((ids[:, None] + 1) // 2 * ids[None, :]) % count) / count
+    is_sine = (ids % 2 == 0) & (ids > 0)
+    basis = np.where(is_sine[:, None], np.sin(angles), np.cos(angles))
+    scaling = np.where((ids == 0) | (ids == count - 1), 1.0 / count, 2.0 / count)
+    forward = basis * scaling[:, None]
+    each = count // shares
+    to_modes = np.zeros((shares, 2, each, 2, count))
+    to_planes = np.zeros((2, count, shares, 2, each))
+    for half in range(2):
+        to_modes[:, half, :, half, :] = forward.T.reshape(shares, each, count)
+        to_planes[half, :, :, half, :] = basis.reshape(count, shares, each)
+    return (
+        split_table(to_modes.reshape(2 * count, 2 * count)),
+        split_table(to_planes.reshape(2 * count, 2 * count)),
+    )
+
+
+def split(value):
+    high = value.astype(jnp.bfloat16)
+    low = (value - high.astype(jnp.float32)).astype(jnp.bfloat16)
+    return high, low
+
+
+def dot(left, right):
+    return jnp.dot(left, right, preferred_element_type=jnp.float32)
+
+
+def label_kernel(onehot_ref, labels_ref):
+    rows = onehot_ref.shape[1]
+    first = lax.broadcasted_iota(jnp.int32, (rows, rows), 0)
+    second = lax.broadcasted_iota(jnp.int32, (rows, rows), 1)
+
+    def step(column, held):
+        held = dot(onehot_ref[column], held).astype(jnp.bfloat16)
+        labels_ref[column] = held
+        return held
+
+    lax.fori_loop(0, onehot_ref.shape[0], step, (first == second).astype(jnp.bfloat16))
+
+
+def chain_kernel(
+    shares, strips, half_cols,
+    recv_ref, sigma_ref, inv_ref, west_ref, east_ref,
+    fhi_ref, flo_ref, bhi_ref, blo_ref,
+    out_ref, x_ref, a_ref, b_ref,
+):
+    columns = x_ref.shape[0]
+    modes = x_ref.shape[2]
+    lane = lax.broadcasted_iota(jnp.int32, (PAD, 3 * PAD), 1)
+
+    def folded(left, right):
+        high, low = split(dot(left, right))
+        return jnp.where(lane < 2 * PAD, high.astype(jnp.float32), low.astype(jnp.float32)).astype(
+            jnp.bfloat16
+        )
+
+    def prepare(column, carry):
+        inverse = inv_ref[column][:, :PAD]
+        a_ref[column] = folded(inverse, west_ref[column])
+        b_ref[column] = folded(inverse, east_ref[jnp.minimum(column + 1, columns - 1)])
+        return carry
+
+    lax.fori_loop(0, columns, prepare, 0, unroll=4)
+
+    def to_modes(strip, carry):
+        planes = jnp.concatenate([recv_ref[share, strip] for share in range(shares)], axis=1)
+        coeffs = dot(planes, fhi_ref[...]) + dot(planes, flo_ref[...])
+        for half in range(2):
+            for place in range(half_cols):
+                own = coeffs[place * NODES : (place + 1) * NODES, half * modes : (half + 1) * modes]
+                own = jnp.concatenate([own, jnp.zeros((PAD - NODES, modes), jnp.float32)], axis=0)
+                high, low = split(own)
+                column = (strip * 2 + half) * half_cols + place
+                x_ref[column] = dot(inv_ref[column], jnp.concatenate([high, low], axis=0))
+        return carry
+
+    lax.fori_loop(0, strips, to_modes, 0)
+
+    sigma = jnp.broadcast_to(sigma_ref[...], (PAD, modes))
+
+    def stacked(value):
+        high, low = split(value)
+        return jnp.concatenate([high, low, high], axis=0)
+
+    def forward(column, previous):
+        value = x_ref[column] - sigma * dot(a_ref[column], stacked(previous))
+        x_ref[column] = value
+        return value
+
+    last = lax.fori_loop(1, columns, forward, x_ref[0])
+
+    def backward(step, following):
+        column = columns - 2 - step
+        value = x_ref[column] - sigma * dot(b_ref[column], stacked(following))
+        x_ref[column] = value
+        return value
+
+    lax.fori_loop(0, columns - 1, backward, last)
+
+    def to_planes(strip, carry):
+        pieces = []
+        for place in range(half_cols):
+            first = x_ref[strip * 2 * half_cols + place]
+            second = x_ref[(strip * 2 + 1) * half_cols + place]
+            pieces.append(jnp.concatenate([first[:NODES], second[:NODES]], axis=1))
+        high, low = split(jnp.concatenate(pieces, axis=0))
+        planes = dot(high, bhi_ref[...]) + dot(low, bhi_ref[...]) + dot(high, blo_ref[...])
+        width = planes.shape[1] // shares
+        for share in range(shares):
+            out_ref[share, strip] = planes[:, share * width : (share + 1) * width].astype(
+                jnp.bfloat16
+            )
+        return carry
+
+    lax.fori_loop(0, strips, to_planes, 0)
+
+
+def chain_on_device(u_field, v_field, sigma, west, dinv, west_coupling, east_coupling):
+    shares, strips = lax.axis_size("plane"), lax.axis_size("strip")
+    planes_dev, columns, flat_width = u_field.shape
+    planes = planes_dev * shares
+    rows = flat_width // NODES
+    half_cols = columns // 2
+    groups = shares // 2
+    all_columns = columns * strips
+    vmem = pl.BlockSpec(memory_space=pltpu.VMEM)
+
+    west_all = lax.all_gather(west, "strip", axis=0, tiled=True)
+    sigma_all = lax.all_gather(sigma, "plane", axis=0, tiled=True)
+    onehots = (west_all[:, :, None] == jnp.arange(rows, dtype=jnp.int32)).astype(jnp.bfloat16)
+    labels_all = pl.pallas_call(
+        label_kernel,
+        out_shape=jax.ShapeDtypeStruct((all_columns, rows, rows), jnp.bfloat16),
+        in_specs=[vmem],
+        out_specs=vmem,
+    )(onehots)
+    labels = lax.dynamic_slice_in_dim(labels_all, lax.axis_index("strip") * columns, columns, 0)
+
+    fields = jnp.stack([u_field, v_field]).reshape(2, planes_dev, columns, rows, NODES)
+    outgoing = jnp.einsum("grc,fzgrn->gcfzn", labels, fields)
+    outgoing = (
+        outgoing.reshape(2, half_cols, groups, strips, 2, planes_dev, NODES)
+        .transpose(2, 4, 3, 1, 6, 0, 5)
+        .reshape(shares * strips, half_cols * NODES, 2 * planes_dev)
+    )
+    received = lax.all_to_all(outgoing, ("plane", "strip"), 0, 0, tiled=True)
+    received = received.reshape(shares, strips, half_cols * NODES, 2 * planes_dev)
+
+    group = lax.axis_index("plane") // 2
+    own = lax.dynamic_slice_in_dim(labels, group * strips, strips, 2)
+    matrices = jnp.stack([dinv, west_coupling, east_coupling])
+    matrices = jnp.einsum("grc,mgre->cmge", own, matrices)
+    matrices = lax.all_to_all(matrices, "strip", 0, 0, tiled=True)
+    matrices = matrices.transpose(1, 0, 2, 3).reshape(3, all_columns, NODES, NODES)
+    spare = PAD - NODES
+    matrices = jnp.pad(matrices, ((0, 0), (0, 0), (0, spare), (0, spare)))
+    inverse = jnp.concatenate([matrices[0]] * 2, axis=2)
+    from_west = jnp.concatenate([matrices[1]] * 3, axis=2)
+    from_east = jnp.concatenate([matrices[2]] * 3, axis=2)
+
+    (fhi, flo), (bhi, blo) = transform_tables(planes, shares)
+    result = pl.pallas_call(
+        lambda *refs: chain_kernel(shares, strips, half_cols, *refs),
+        out_shape=jax.ShapeDtypeStruct(received.shape, jnp.bfloat16),
+        in_specs=[vmem] * 9,
+        out_specs=vmem,
+        scratch_shapes=[
+            pltpu.VMEM((all_columns, PAD, planes), jnp.float32),
+            pltpu.VMEM((all_columns, PAD, 3 * PAD), jnp.bfloat16),
+            pltpu.VMEM((all_columns, PAD, 3 * PAD), jnp.bfloat16),
+        ],
+        compiler_params=pltpu.CompilerParams(vmem_limit_bytes=48 * 1024 * 1024),
+    )(received, sigma_all.reshape(1, planes), inverse, from_west, from_east, fhi, flo, bhi, blo)
+
+    returned = lax.all_to_all(
+        result.reshape(shares * strips, half_cols * NODES, 2 * planes_dev),
+        ("plane", "strip"), 0, 0, tiled=True,
+    )
+    returned = returned.reshape(groups, 2, strips, half_cols, NODES, 2, planes_dev)
+    returned = returned.transpose(5, 3, 0, 2, 1, 6, 4).reshape(
+        columns, rows, 2, planes_dev, NODES
+    )
+    outs = jnp.einsum("grc,gcfzn->fzgrn", labels, returned).reshape(
+        2, planes_dev, columns, flat_width
+    )
+    return outs[0], outs[1]
+
+
 def solution(mesh):
     in_specs = (
         P("plane", "strip", None),
@@ -185,6 +388,8 @@
         P("strip", None, None),
     )
     out_specs = (P("plane", "strip", None), P("plane", "strip", None))
+    spread = mesh.shape["plane"] % 2 == 0 and mesh.shape["plane"] * mesh.shape["strip"] == 32
+    body = chain_on_device if spread else strip_chain_on_device
     return jax.shard_map(
-        on_device, mesh=mesh, in_specs=in_specs, out_specs=out_specs, check_vma=False
-    )
+        body, mesh=mesh, in_specs=in_specs, out_specs=out_specs, check_vma=False
+    )

time: 762 us -> 173 us (0.23)
  waiting for transfers between devices: 462 us -> 13.2 us
  starting transfers between devices: 165 us -> 18.4 us
  blocking collectives: 0 us -> 63.4 us
  matrix products: 57.1 us -> 5.56 us
  Pallas kernels: 0 us -> 39.4 us
  local copies, waits for them, and re-layouts: 59.3 us -> 23.7 us
    ppermute x16 -> x0, waiting for transfers between devices: 407 us -> none  [from_behind(): return lax.ppermute(block, axis, route)]
    ppermute x16 -> x0, starting transfers between devices: 110 us -> none  [from_behind(): return lax.ppermute(block, axis, route)]
    dot_general x52 -> x3, matrix products: 57.1 us -> 5.56 us  [the longest x1 2.36 us: chain_on_device(): outgoing = jnp.einsum('grc,fzgrn->gcfzn', labels, fields)]
    all_to_all x8 -> x2, waiting for transfers between devices: 55.1 us -> 13.2 us  [the longest x1 13.2 us: chain_on_device(): received = lax.all_to_all(outgoing, ('plane', 'strip'), 0, 0, tiled=True)]
    pallas_call x0 -> x2, Pallas kernels: none -> 39.4 us  [the longest x1 30.2 us: chain_on_device(): pl.pallas_call(lambda *refs: chain_kernel(shares, strips, half_cols, *ref...]
    all_to_all x8 -> x2, starting transfers between devices: 55.3 us -> 18.4 us  [the longest x1 13.2 us: chain_on_device(): received = lax.all_to_all(outgoing, ('plane', 'strip'), 0, 0, tiled=True)]
    all_to_all x0 -> x1, blocking collectives: none -> 32.5 us  [chain_on_device(): lax.all_to_all(result.reshape(shares * strips, half_cols * NODES, 2 * pla...]
    all_gather x0 -> x1, blocking collectives: none -> 24.5 us  [chain_on_device(): west_all = lax.all_gather(west, 'strip', axis=0, tiled=True)]
  transfers between devices with their start and end apart: 24 -> 2, of which waited for: 24 -> 1; matrix products, arithmetic and copies ran while one was open for 5% -> 12% of each run, Pallas kernels for 0% -> 0%
where the time goes in v1:
time: 173 us; the launch traced here: 170 us
  blocking collectives  63.4 us (37%)
  Pallas kernels  39.4 us (23%)
  local copies, waits for them, and re-layouts  23.7 us (14%)
  starting transfers between devices  18.4 us (11%)
  waiting for transfers between devices  13.2 us (8%)
  matrix products  5.56 us (3%)
  other arithmetic  5.14 us (3%)
    all_to_all x1, blocking collectives, chain_on_device(): lax.all_to_all(result.reshape(shares * strips, half_cols * NODES, 2 * pla...  32.5 us
    pallas_call x1, Pallas kernels, chain_on_device(): pl.pallas_call(lambda *refs: chain_kernel(shares, strips, half_cols, *ref...  30.2 us
    all_gather x1, blocking collectives, chain_on_device(): west_all = lax.all_gather(west, 'strip', axis=0, tiled=True)  24.5 us
    all_to_all x1, waiting for transfers between devices, chain_on_device(): received = lax.all_to_all(outgoing, ('plane', 'strip'), 0, 0, tiled=True)  13.2 us
    all_to_all x1, starting transfers between devices, chain_on_device(): received = lax.all_to_all(outgoing, ('plane', 'strip'), 0, 0, tiled=True)  13.2 us
    unnamed x23, local copies, waits for them, and re-layouts  9.43 us
    pallas_call x1, Pallas kernels, chain_on_device(): pl.pallas_call(label_kernel, out_shape=jax.ShapeDtypeStruct((all_columns,...  9.24 us
    unnamed x1, blocking collectives  6.3 us
  transfers between devices with their start and end apart: 2, of which 1 were waited for; matrix products, arithmetic and copies ran while one was open for 12% of the time, Pallas kernels for 0%

profile of v1, /device:TPU:5, one launch (start us, length us, event | category | flops | bytes accessed | tf_op | source)
XLA Modules:
  0.0 170.4 jit_solution(8754069400175955167)
XLA Ops:
  0.7 24.5 %all_gather.6 = s32[64,16]{1,0:T(8,128)S(1)} all-gather(s32[8,16]{1,0:T(8,128)} %param.14), channel_id=1, replica_groups=mesh['plane'=4,'strip'=8] {'strip'}, dimensions={0}, use_global_device_ids=true | all-gather | bytes 4608 | tf_op jit(solution)/shard_map/all_gather | solution.py:319
  25.2 0.9 fusion.12.onehot_ref
  26.1 9.2 %shard_map.122 = bf16[64,16,16]{2,1,0:T(8,128)(2,1)} custom-call(bf16[64,16,16]{2,1,0:T(8,128)(2,1)} %fusion.12.onehot_ref), custom_call_target="tpu_custom_call" | custom-call | tf_op jit(solution)/shard_map/pallas_call | solution.py:322
  35.3 1.7 convolution_bitcast_fusion
  37.0 0.0 copy-start.4
  37.0 0.9 copy.52
  37.9 5.2 %all-to-all-start.1 = ((bf16[8,3,8,1296]{3,2,1,0:T(8,128)(2,1)}), bf16[8,3,8,1296]{3,2,1,0:T(8,128)(2,1)S(1)}, u32[]{:S(2)}, u32[]{:S(2)}) async-start(bf16[8,3,8,1296]{3,2,1,0:T(8,128)(2,1)} %copy.52), calls=%async_computation.1 | async-start | bytes 1081344 | tf_op jit(solution)/shard_map/all_to_all | solution.py:344
  43.1 0.0 copy-done.4
  43.1 1.4 copy.45
  44.5 0.0 copy-start.5
  44.5 0.5 copy.47
  45.0 0.6 copy-done.5
  45.6 1.4 copy.46
  47.0 0.5 copy.48
  47.5 2.4 %fusion = bf16[8,16,2,64,36]{3,1,4,2,0:T(8,128)(2,1)S(1)} fusion(bf16[1,64,8,16,36]{1,3,4,0,2:T(8,128)(2,1)S(1)} %copy.48, bf16[1,64,8,16,36]{1,3,4,0,2:T(8,128)(2,1)S(1)} %copy.47, bf16[64,16,16]{2,1,0:T(8,128)(2,1)} %shard_map.122, s32[]{:T(128)S(6)} %select_n.15), kind=kOutput, calls=%fused_computation.1 | convolution fusion | flops 21233664 | bytes 2392068 | tf_op jit(solution)/shard_map/grc,fzgrn->gcfzn/dot_general | solution.py:331
  49.9 2.4 %copy.50 = bf16[2,2,8,4,36,2,64]{6,5,4,3,2,1,0:T(2,128)(2,1)S(1)} copy(bf16[2,2,8,4,36,2,64]{6,2,0,4,1,3,5:T(8,128)(2,1)S(1)} %bitcast.50) | data formatting | bytes 2359296 | tf_op jit(solution)/shard_map/transpose | solution.py:334
  52.3 2.2 %reshape.40 = bf16[32,144,128]{2,1,0:T(8,128)(2,1)} reshape(bf16[2,2,8,4,36,2,64]{6,5,4,3,2,1,0:T(2,128)(2,1)S(1)} %copy.50) | data formatting | bytes 2359296 | tf_op jit(solution)/shard_map/reshape | solution.py:335
  54.5 0.0 all-to-all-done.1
  54.5 13.2 %all-to-all-start = ((bf16[32,144,128]{2,1,0:T(8,128)(2,1)}), bf16[32,144,128]{2,1,0:T(8,128)(2,1)S(1)}, u32[]{:S(2)}, u32[]{:S(2)}) async-start(bf16[32,144,128]{2,1,0:T(8,128)(2,1)} %reshape.40), calls=%async_computation | async-start | bytes 2359296 | tf_op jit(solution)/shard_map/all_to_all | solution.py:337
  67.8 0.0 copy-done.7
  67.8 0.6 dynamic-slice
  69.0 0.0 copy-done.6
  69.0 0.2 dynamic-update-slice
  69.3 6.3 %all-reduce.1 = f32[256]{0:T(256)S(1)} all-reduce(f32[256]{0:T(256)S(1)} %dynamic-update-slice), channel_id=1, replica_groups=mesh['plane'=4,'strip'=8] {'plane'}, use_global_device_ids=true, to_apply=%add.1 | all-reduce | flops 256 | bytes 2048
  75.6 0.8 copy.53
  76.4 2.7 %reshape.43 = bf16[3,64,36,36]{3,2,1,0:T(8,128)(2,1)S(1)} reshape(bf16[3,8,8,1296]{3,2,1,0:T(8,128)(2,1)} %copy.53) | data formatting | bytes 995328 | tf_op jit(solution)/shard_map/reshape | solution.py:345
  79.1 0.5 fusion.11
  79.6 0.4 pad_maximum_fusion.2.refs_2_
  80.0 0.0 copy-start
  80.0 0.0 copy-start.1
  80.1 0.0 copy-start.2
  80.1 3.8 %pad_maximum_fusion = (bf16[64,48,144]{2,1,0:T(8,128)(2,1)}, bf16[64,48,144]{2,1,0:T(8,128)(2,1)}) fusion(bf16[64,48,48]{2,1,0:T(8,128)(2,1)S(1)} %get-tuple-element.11, bf16[64,48,48]{2,1,0:T(8,128)(2,1)S(1)} %get-tuple-element.10), kind=kLoop, calls=%fused_computation.9 | loop fusion | flops 5308416 | bytes 2359296 | tf_op jit(solution)/shard_map/concatenate | solution.py:349
  83.9 13.2 %all-to-all-done = bf16[32,144,128]{2,1,0:T(8,128)(2,1)S(1)} async-done(((bf16[32,144,128]{2,1,0:T(8,128)(2,1)}), bf16[32,144,128]{2,1,0:T(8,128)(2,1)S(1)}, u32[]{:S(2)}, u32[]{:S(2)}) %all-to-all-start) | async-done | bytes 1179680 | tf_op jit(solution)/shard_map/all_to_all | solution.py:337
  97.1 0.0 copy-done
  97.1 0.0 copy-done.1
  97.1 0.0 copy-done.2
  97.1 0.0 copy-start.3
  97.1 1.0 copy-done.3
  98.2 30.2 %shard_map.123 = bf16[4,8,144,128]{3,2,1,0:T(8,128)(2,1)S(1)} custom-call(bf16[4,8,144,128]{3,2,1,0:T(8,128)(2,1)S(1)} %bitcast.46, f32[1,256]{1,0:T(1,128)S(1)} %bitcast.48, bf16[64,48,96]{2,1,0:T(8,128)(2,1)S(1)} %pad_maximum_fusion.2.refs_2_, bf16[64,48,144]{2,1,0:T(8,128)(2,1)} %get-tuple-element.13.refs_3_, ...), custom_call_target="tpu_custom_call" | custom-call | tf_op jit(solution)/shard_map/pallas_call | solution.py:353
  128.4 32.5 %all_to_all.15 = bf16[32,144,128]{2,1,0:T(8,128)(2,1)S(1)} all-to-all(bf16[32,144,128]{2,1,0:T(8,128)(2,1)S(1)} %bitcast.47), channel_id=1, replica_groups=mesh['plane'=4,'strip'=8] {'plane','strip'}, dimensions={0} | all-to-all | bytes 2359296 | tf_op jit(solution)/shard_map/all_to_all | solution.py:366
  160.9 1.0 reshape.45
  162.0 0.9 copy.54
  162.9 1.5 convolution_bitcast_fusion.1
  164.4 0.4 fusion.24
  164.8 0.8 copy.56
  165.6 2.0 %copy.58 = bf16[64,8,576]{2,1,0:T(8,128)(2,1)} copy(bf16[64,8,576]{0,1,2:T(8,128)(2,1)S(1)} %bitcast.51) | data formatting | bytes 1179648
  167.6 0.8 copy.55
  168.4 2.0 %copy.57 = bf16[64,8,576]{2,1,0:T(8,128)(2,1)} copy(bf16[64,8,576]{0,1,2:T(8,128)(2,1)S(1)} %bitcast.52) | data formatting | bytes 1179648
  (3 shorter events, 0.0 us)
Async XLA Ops:
  37.0 6.1 %copy-start.4 = (bf16[64,8,576]{2,1,0:T(8,128)(2,1)S(1)}, bf16[64,8,576]{2,1,0:T(8,128)(2,1)}, u32[]{:S(2)}) copy-start(bf16[64,8,576]{2,1,0:T(8,128)(2,1)} %param.11) | copy-start | bytes 1769476
  37.9 16.7 %all-to-all-start.1 = ((bf16[8,3,8,1296]{3,2,1,0:T(8,128)(2,1)}), bf16[8,3,8,1296]{3,2,1,0:T(8,128)(2,1)S(1)}, u32[]{:S(2)}, u32[]{:S(2)}) async-start(bf16[8,3,8,1296]{3,2,1,0:T(8,128)(2,1)} %copy.52), calls=%async_computation.1 | async-start | bytes 1081344 | tf_op jit(solution)/shard_map/all_to_all | solution.py:344
  44.5 1.1 copy-start.5
  54.5 13.2 %copy-start.7 = (u32[32]{0:T(128)S(1)}, u32[32]{0:T(128)}, u32[]{:S(2)}) copy-start(u32[32]{0:T(128)} %constant.63) | copy-start | bytes 388
  54.5 14.5 %copy-start.6 = (f32[64]{0:T(128)S(1)}, f32[64]{0:T(128)}, u32[]{:S(2)}) copy-start(f32[64]{0:T(128)} %param.13) | copy-start | bytes 772
  54.5 42.6 %all-to-all-start = ((bf16[32,144,128]{2,1,0:T(8,128)(2,1)}), bf16[32,144,128]{2,1,0:T(8,128)(2,1)S(1)}, u32[]{:S(2)}, u32[]{:S(2)}) async-start(bf16[32,144,128]{2,1,0:T(8,128)(2,1)} %reshape.40), calls=%async_computation | async-start | bytes 2359296 | tf_op jit(solution)/shard_map/all_to_all | solution.py:337
  80.0 17.1 %copy-start = (bf16[512,512]{1,0:T(8,128)(2,1)S(1)}, bf16[512,512]{1,0:T(8,128)(2,1)}, u32[]{:S(2)}) copy-start(bf16[512,512]{1,0:T(8,128)(2,1)} %constant.58.clone.refs_8_) | copy-start | bytes 1572868
  80.0 17.1 %copy-start.1 = (bf16[512,512]{1,0:T(8,128)(2,1)S(1)}, bf16[512,512]{1,0:T(8,128)(2,1)}, u32[]{:S(2)}) copy-start(bf16[512,512]{1,0:T(8,128)(2,1)} %constant.57.clone.refs_7_) | copy-start | bytes 1572868
  80.1 17.1 %copy-start.2 = (bf16[512,512]{1,0:T(8,128)(2,1)S(1)}, bf16[512,512]{1,0:T(8,128)(2,1)}, u32[]{:S(2)}) copy-start(bf16[512,512]{1,0:T(8,128)(2,1)} %constant.56.clone.refs_6_) | copy-start | bytes 1572868
  97.1 1.0 copy-start.3

commit v2 on v1

--- a/solution.py
+++ b/solution.py
@@ -216,25 +216,107 @@
     return jnp.dot(left, right, preferred_element_type=jnp.float32)
 
 
-def label_kernel(onehot_ref, labels_ref):
-    rows = onehot_ref.shape[1]
-    first = lax.broadcasted_iota(jnp.int32, (rows, rows), 0)
-    second = lax.broadcasted_iota(jnp.int32, (rows, rows), 1)
-
-    def step(column, held):
+def label_kernel(
+    onehot_ref, sigma_ref, labels_ref, sigmas_ref,
+    local_ref, total_ref, totals_ref, strip_send, strip_recv, plane_send, plane_recv,
+):
+    columns, rows, _ = onehot_ref.shape
+    shares, strips = sigmas_ref.shape[0], totals_ref.shape[0]
+    my_share, my_strip = lax.axis_index("plane"), lax.axis_index("strip")
+
+    barrier = pltpu.get_barrier_semaphore()
+    for step in range(1, strips):
+        pl.semaphore_signal(
+            barrier, 1, device_id={"plane": my_share, "strip": (my_strip + step) % strips}
+        )
+    for step in range(1, shares):
+        pl.semaphore_signal(
+            barrier, 1, device_id={"plane": (my_share + step) % shares, "strip": my_strip}
+        )
+
+    start = (
+        lax.broadcasted_iota(jnp.int32, (rows, 128), 0)
+        == lax.broadcasted_iota(jnp.int32, (rows, 128), 1)
+    ).astype(jnp.bfloat16)
+    held = start
+    for column in range(columns):
         held = dot(onehot_ref[column], held).astype(jnp.bfloat16)
-        labels_ref[column] = held
-        return held
-
-    lax.fori_loop(0, onehot_ref.shape[0], step, (first == second).astype(jnp.bfloat16))
+        local_ref[column] = held
+    total_ref[...] = held
+    pl.semaphore_wait(barrier, strips + shares - 2)
+
+    def strip_copy(step, slot):
+        return pltpu.make_async_remote_copy(
+            src_ref=total_ref,
+            dst_ref=totals_ref.at[slot],
+            send_sem=strip_send.at[step],
+            recv_sem=strip_recv.at[slot],
+            device_id={"plane": my_share, "strip": (my_strip + step) % strips},
+        )
+
+    def plane_copy(step, slot):
+        return pltpu.make_async_remote_copy(
+            src_ref=sigma_ref,
+            dst_ref=sigmas_ref.at[slot],
+            send_sem=plane_send.at[step],
+            recv_sem=plane_recv.at[slot],
+            device_id={"plane": (my_share + step) % shares, "strip": my_strip},
+        )
+
+    for step in range(1, strips):
+        strip_copy(step, my_strip).start()
+    for step in range(1, shares):
+        plane_copy(step, my_share).start()
+    totals_ref[my_strip] = held
+    sigmas_ref[my_share] = sigma_ref[...]
+    for step in range(1, strips):
+        strip_copy(step, (my_strip + strips - step) % strips).wait_recv()
+    before = start
+    for strip in range(strips - 1):
+        joined = dot(totals_ref[strip][:, :rows], before)
+        before = jnp.where(strip < my_strip, joined, before.astype(jnp.float32)).astype(
+            jnp.bfloat16
+        )
+    for column in range(columns):
+        labels_ref[column] = dot(local_ref[column][:, :rows], before).astype(jnp.bfloat16)
+    for step in range(1, shares):
+        plane_copy(step, (my_share + shares - step) % shares).wait_recv()
+    for step in range(1, strips):
+        strip_copy(step, my_strip).wait_send()
+    for step in range(1, shares):
+        plane_copy(step, my_share).wait_send()
 
 
 def chain_kernel(
     shares, strips, half_cols,
     recv_ref, sigma_ref, inv_ref, west_ref, east_ref,
     fhi_ref, flo_ref, bhi_ref, blo_ref,
-    out_ref, x_ref, a_ref, b_ref,
+    out_ref, x_ref, a_ref, b_ref, planes_ref, send_sems, recv_sems, own_sem,
 ):
+    my_share, my_strip = lax.axis_index("plane"), lax.axis_index("strip")
+    me = my_share * strips + my_strip
+    devices = shares * strips
+
+    barrier = pltpu.get_barrier_semaphore()
+
+    def greet(step, carry):
+        other = (me + step) % devices
+        pl.semaphore_signal(
+            barrier, 1, device_id={"plane": other // strips, "strip": other % strips}
+        )
+        return carry
+
+    lax.fori_loop(1, devices, greet, 0)
+
+    def result_copy(share, strip, slot):
+        return pltpu.make_async_remote_copy(
+            src_ref=planes_ref.at[share * strips + strip],
+            dst_ref=out_ref.at[slot],
+            send_sem=send_sems.at[share * strips + strip],
+            recv_sem=recv_sems.at[slot],
+            device_id={"plane": share, "strip": strip},
+        )
+
     columns = x_ref.shape[0]
     modes = x_ref.shape[2]
     lane = lax.broadcasted_iota(jnp.int32, (PAD, 3 * PAD), 1)
@@ -253,57 +335,72 @@
 
     lax.fori_loop(0, columns, prepare, 0, unroll=4)
 
-    def to_modes(strip, carry):
+    sigma = jnp.broadcast_to(sigma_ref[...], (PAD, modes))
+
+    def stacked(value):
+        high, low = split(value)
+        return jnp.concatenate([high, low, high], axis=0)
+
+    def forward(strip, previous):
         planes = jnp.concatenate([recv_ref[share, strip] for share in range(shares)], axis=1)
         coeffs = dot(planes, fhi_ref[...]) + dot(planes, flo_ref[...])
+        sources = []
         for half in range(2):
             for place in range(half_cols):
                 own = coeffs[place * NODES : (place + 1) * NODES, half * modes : (half + 1) * modes]
                 own = jnp.concatenate([own, jnp.zeros((PAD - NODES, modes), jnp.float32)], axis=0)
                 high, low = split(own)
                 column = (strip * 2 + half) * half_cols + place
-                x_ref[column] = dot(inv_ref[column], jnp.concatenate([high, low], axis=0))
-        return carry
-
-    lax.fori_loop(0, strips, to_modes, 0)
-
-    sigma = jnp.broadcast_to(sigma_ref[...], (PAD, modes))
-
-    def stacked(value):
-        high, low = split(value)
-        return jnp.concatenate([high, low, high], axis=0)
-
-    def forward(column, previous):
-        value = x_ref[column] - sigma * dot(a_ref[column], stacked(previous))
-        x_ref[column] = value
-        return value
-
-    last = lax.fori_loop(1, columns, forward, x_ref[0])
+                sources.append(dot(inv_ref[column], jnp.concatenate([high, low], axis=0)))
+        for place in range(2 * half_cols):
+            column = strip * 2 * half_cols + place
+            previous = sources[place] - sigma * dot(a_ref[column], stacked(previous))
+            x_ref[column] = previous
+        return previous
+
+    nothing = jnp.zeros((PAD, modes), jnp.float32)
+    lax.fori_loop(0, strips, forward, nothing)
+    pl.semaphore_wait(barrier, devices - 1)
 
     def backward(step, following):
-        column = columns - 2 - step
-        value = x_ref[column] - sigma * dot(b_ref[column], stacked(following))
-        x_ref[column] = value
-        return value
-
-    lax.fori_loop(0, columns - 1, backward, last)
-
-    def to_planes(strip, carry):
-        pieces = []
-        for place in range(half_cols):
-            first = x_ref[strip * 2 * half_cols + place]
-            second = x_ref[(strip * 2 + 1) * half_cols + place]
-            pieces.append(jnp.concatenate([first[:NODES], second[:NODES]], axis=1))
+        strip = strips - 1 - step
+        solved = [None] * (2 * half_cols)
+        for place in reversed(range(2 * half_cols)):
+            column = strip * 2 * half_cols + place
+            following = x_ref[column] - sigma * dot(b_ref[column], stacked(following))
+            solved[place] = following
+        pieces = [
+            jnp.concatenate([solved[place][:NODES], solved[half_cols + place][:NODES]], axis=1)
+            for place in range(half_cols)
+        ]
         high, low = split(jnp.concatenate(pieces, axis=0))
         planes = dot(high, bhi_ref[...]) + dot(low, bhi_ref[...]) + dot(high, blo_ref[...])
         width = planes.shape[1] // shares
         for share in range(shares):
-            out_ref[share, strip] = planes[:, share * width : (share + 1) * width].astype(
-                jnp.bfloat16
-            )
+            planes_ref[share * strips + strip] = planes[
+                :, share * width : (share + 1) * width
+            ].astype(jnp.bfloat16)
+        for share in range(shares):
+            mine = (share == my_share) & (strip == my_strip)
+
+            @pl.when(jnp.logical_not(mine))
+            def _():
+                result_copy(share, strip, me).start()
+
+        return following
+
+    lax.fori_loop(0, strips, backward, nothing)
+    own_copy = pltpu.make_async_copy(planes_ref.at[me], out_ref.at[me], own_sem)
+    own_copy.start()
+    own_copy.wait()
+
+    def finish(step, carry):
+        source = (me + step) % devices
+        result_copy(source // strips, source % strips, source).wait_recv()
+        result_copy(source // strips, source % strips, me).wait_send()
         return carry
 
-    lax.fori_loop(0, strips, to_planes, 0)
+    lax.fori_loop(1, devices, finish, 0)
 
 
 def chain_on_device(u_field, v_field, sigma, west, dinv, west_coupling, east_coupling):
@@ -316,16 +413,29 @@
     all_columns = columns * strips
     vmem = pl.BlockSpec(memory_space=pltpu.VMEM)
 
-    west_all = lax.all_gather(west, "strip", axis=0, tiled=True)
-    sigma_all = lax.all_gather(sigma, "plane", axis=0, tiled=True)
-    onehots = (west_all[:, :, None] == jnp.arange(rows, dtype=jnp.int32)).astype(jnp.bfloat16)
-    labels_all = pl.pallas_call(
+    onehots = (west[:, :, None] == jnp.arange(rows, dtype=jnp.int32)).astype(jnp.bfloat16)
+    sigma_tile = jnp.broadcast_to(jnp.pad(sigma, (0, 128 - planes_dev))[None], (8, 128))
+    labels, sigma_tiles = pl.pallas_call(
         label_kernel,
-        out_shape=jax.ShapeDtypeStruct((all_columns, rows, rows), jnp.bfloat16),
-        in_specs=[vmem],
-        out_specs=vmem,
-    )(onehots)
-    labels = lax.dynamic_slice_in_dim(labels_all, lax.axis_index("strip") * columns, columns, 0)
+        out_shape=(
+            jax.ShapeDtypeStruct((columns, rows, 128), jnp.bfloat16),
+            jax.ShapeDtypeStruct((shares, 8, 128), jnp.float32),
+        ),
+        in_specs=[vmem] * 2,
+        out_specs=(vmem, vmem),
+        scratch_shapes=[
+            pltpu.VMEM((columns, rows, 128), jnp.bfloat16),
+            pltpu.VMEM((rows, 128), jnp.bfloat16),
+            pltpu.VMEM((strips, rows, 128), jnp.bfloat16),
+            pltpu.SemaphoreType.DMA((strips,)),
+            pltpu.SemaphoreType.DMA((strips,)),
+            pltpu.SemaphoreType.DMA((shares,)),
+            pltpu.SemaphoreType.DMA((shares,)),
+        ],
+        compiler_params=pltpu.CompilerParams(collective_id=0, has_side_effects=True),
+    )(onehots, sigma_tile)
+    labels = labels[:, :, :rows]
+    sigma_all = sigma_tiles[:, 0, :planes_dev].reshape(planes)
 
     fields = jnp.stack([u_field, v_field]).reshape(2, planes_dev, columns, rows, NODES)
     outgoing = jnp.einsum("grc,fzgrn->gcfzn", labels, fields)
@@ -352,22 +462,24 @@
     (fhi, flo), (bhi, blo) = transform_tables(planes, shares)
     result = pl.pallas_call(
         lambda *refs: chain_kernel(shares, strips, half_cols, *refs),
-        out_shape=jax.ShapeDtypeStruct(received.shape, jnp.bfloat16),
+        out_shape=jax.ShapeDtypeStruct(outgoing.shape, jnp.bfloat16),
         in_specs=[vmem] * 9,
         out_specs=vmem,
         scratch_shapes=[
             pltpu.VMEM((all_columns, PAD, planes), jnp.float32),
             pltpu.VMEM((all_columns, PAD, 3 * PAD), jnp.bfloat16),
             pltpu.VMEM((all_columns, PAD, 3 * PAD), jnp.bfloat16),
+            pltpu.VMEM(outgoing.shape, jnp.bfloat16),
+            pltpu.SemaphoreType.DMA((shares * strips,)),
+            pltpu.SemaphoreType.DMA((shares * strips,)),
+            pltpu.SemaphoreType.DMA,
         ],
-        compiler_params=pltpu.CompilerParams(vmem_limit_bytes=48 * 1024 * 1024),
+        compiler_params=pltpu.CompilerParams(
+            vmem_limit_bytes=48 * 1024 * 1024, collective_id=1, has_side_effects=True
+        ),
     )(received, sigma_all.reshape(1, planes), inverse, from_west, from_east, fhi, flo, bhi, blo)
 
-    returned = lax.all_to_all(
-        result.reshape(shares * strips, half_cols * NODES, 2 * planes_dev),
-        ("plane", "strip"), 0, 0, tiled=True,
-    )
-    returned = returned.reshape(groups, 2, strips, half_cols, NODES, 2, planes_dev)
+    returned = result.reshape(groups, 2, strips, half_cols, NODES, 2, planes_dev)
     returned = returned.transpose(5, 3, 0, 2, 1, 6, 4).reshape(
         columns, rows, 2, planes_dev, NODES
     )

time: 173 us -> 135 us (0.78)
  blocking collectives: 63.4 us -> 0 us
  Pallas kernels: 39.4 us -> 61.6 us
  waiting for transfers between devices: 13.2 us -> 21.1 us
  starting transfers between devices: 18.4 us -> 12.8 us
  local copies, waits for them, and re-layouts: 23.7 us -> 28.4 us
  matrix products: 5.56 us -> 3.52 us
    all_to_all x1 -> x0, blocking collectives: 32.5 us -> none  [chain_on_device(): lax.all_to_all(result.reshape(shares * strips, half_cols * NODES, 2 * pla...]
    all_gather x1 -> x0, blocking collectives: 24.5 us -> none  [chain_on_device(): west_all = lax.all_gather(west, 'strip', axis=0, tiled=True)]
    pallas_call x1, Pallas kernels: 30.2 us -> 52.8 us  [chain_on_device(): pl.pallas_call(lambda *refs: chain_kernel(shares, strips, half_cols, *ref...]
    all_to_all x1, waiting for transfers between devices: 13.2 us -> 20.3 us  [chain_on_device(): received = lax.all_to_all(outgoing, ('plane', 'strip'), 0, 0, tiled=True)]
    unnamed x1 -> x0, blocking collectives: 6.3 us -> none
    all_to_all x1, starting transfers between devices: 13.2 us -> 8.09 us  [chain_on_device(): received = lax.all_to_all(outgoing, ('plane', 'strip'), 0, 0, tiled=True)]
    unnamed x23 -> x20, local copies, waits for them, and re-layouts: 9.43 us -> 12 us
  transfers between devices with their start and end apart: 2 -> 2, of which waited for: 1 -> 2; matrix products, arithmetic and copies ran while one was open for 12% -> 14% of each run, Pallas kernels for 0% -> 0%
where the time goes in v2:
time: 135 us; the launch traced here: 134 us
  Pallas kernels  61.6 us (46%)
  local copies, waits for them, and re-layouts  28.4 us (21%)
  waiting for transfers between devices  21.1 us (16%)
  starting transfers between devices  12.8 us (9%)
  other arithmetic  5.63 us (4%)
  matrix products  3.52 us (3%)
    pallas_call x1, Pallas kernels, chain_on_device(): pl.pallas_call(lambda *refs: chain_kernel(shares, strips, half_cols, *ref...  52.8 us
    all_to_all x1, waiting for transfers between devices, chain_on_device(): received = lax.all_to_all(outgoing, ('plane', 'strip'), 0, 0, tiled=True)  20.3 us
    unnamed x20, local copies, waits for them, and re-layouts  12 us
    pallas_call x1, Pallas kernels, chain_on_device(): pl.pallas_call(label_kernel, out_shape=(jax.ShapeDtypeStruct((columns, ro...  8.77 us
    all_to_all x1, starting transfers between devices, chain_on_device(): received = lax.all_to_all(outgoing, ('plane', 'strip'), 0, 0, tiled=True)  8.09 us
    all_to_all x1, starting transfers between devices, chain_on_device(): matrices = lax.all_to_all(matrices, 'strip', 0, 0, tiled=True)  4.7 us
    concatenate x1, other arithmetic, chain_on_device(): from_west = jnp.concatenate([matrices[1]] * 3, axis=2)  3.81 us
  transfers between devices with their start and end apart: 2, of which 2 were waited for; matrix products, arithmetic and copies ran while one was open for 14% of the time, Pallas kernels for 0%

profile of v2, /device:TPU:5, one launch (start us, length us, event | category | flops | bytes accessed | tf_op | source)
XLA Modules:
  0.0 133.9 jit_solution(15043796288788537187)
XLA Ops:
  0.6 1.4 %fusion.12.onehot_ref = bf16[8,16,16]{2,1,0:T(8,128)(2,1)} fusion(s32[8,16]{1,0:T(8,128)} %param.14), kind=kLoop, calls=%fused_computation.21 | loop fusion | flops 4096 | bytes 4608 | tf_op jit(solution)/shard_map/convert_element_type | solution.py:416
  2.0 0.7 pad.8
  2.7 0.6 broadcast_in_dim.2.sigma_ref
  3.3 8.8 %shard_map.122 = (bf16[8,16,128]{2,1,0:T(8,128)(2,1)}, f32[4,8,128]{2,1,0:T(8,128)}) custom-call(bf16[8,16,16]{2,1,0:T(8,128)(2,1)} %fusion.12.onehot_ref, f32[8,128]{1,0:T(8,128)} %broadcast_in_dim.2.sigma_ref), custom_call_target="tpu_custom_call" | custom-call | tf_op jit(solution)/shard_map/pallas_call | solution.py:418
  12.1 1.7 %convolution_bitcast_fusion = bf16[8,3,8,1296]{3,0,1,2:T(8,128)(2,1)S(1)} fusion(bf16[1,8,16,1296]{3,2,0,1:T(8,128)(2,1)} %bitcast.53, bf16[1,8,16,1296]{3,2,0,1:T(8,128)(2,1)} %bitcast.54, bf16[1,8,16,1296]{3,2,0,1:T(8,128)(2,1)} %bitcast.55, bf16[8,16,16]{2,1,0:T(8,128)(2,1)} %bitcast.52, s32[]{:T(128)S(6)} %select_n.9), kind=kOutput, calls=%fused_computation | convolution fusion | flops 8957952 | bytes 1497092 | tf_op jit(solution)/shard_map/grc,mgre->cmge/dot_general | solution.py:453
  13.8 0.0 copy-start.4
  13.8 0.9 copy.52
  14.7 4.7 %all-to-all-start.1 = ((bf16[8,3,8,1296]{3,2,1,0:T(8,128)(2,1)}), bf16[8,3,8,1296]{3,2,1,0:T(8,128)(2,1)S(1)}, u32[]{:S(2)}, u32[]{:S(2)}) async-start(bf16[8,3,8,1296]{3,2,1,0:T(8,128)(2,1)} %copy.52), calls=%async_computation.1 | async-start | bytes 1081344 | tf_op jit(solution)/shard_map/all_to_all | solution.py:454
  19.4 0.0 copy-done.4
  19.4 1.4 %copy.45 = bf16[64,8,576]{0,1,2:T(8,128)(2,1)S(1)} copy(bf16[64,8,576]{2,1,0:T(8,128)(2,1)S(1)} %copy-done.4) | data formatting | bytes 1179648 | tf_op args[0]
  20.8 0.0 copy-start.5
  20.8 0.5 copy.47
  21.3 0.6 copy-done.5
  21.9 1.4 %copy.46 = bf16[64,8,576]{0,1,2:T(8,128)(2,1)S(1)} copy(bf16[64,8,576]{2,1,0:T(8,128)(2,1)S(1)} %copy-done.5) | data formatting | bytes 1179648 | tf_op args[1]
  23.3 0.0 copy-start.6
  23.3 0.5 copy.48
  23.8 0.3 copy-done.6
  24.1 1.1 fusion
  25.2 2.4 %copy.50 = bf16[2,2,8,4,36,2,64]{6,5,4,3,2,1,0:T(2,128)(2,1)S(1)} copy(bf16[2,2,8,4,36,2,64]{6,2,0,4,1,3,5:T(8,128)(2,1)S(1)} %bitcast.44) | data formatting | bytes 2359296 | tf_op jit(solution)/shard_map/transpose | solution.py:444
  27.6 2.2 %reshape.35 = bf16[32,144,128]{2,1,0:T(8,128)(2,1)} reshape(bf16[2,2,8,4,36,2,64]{6,5,4,3,2,1,0:T(2,128)(2,1)S(1)} %copy.50) | data formatting | bytes 2359296 | tf_op jit(solution)/shard_map/reshape | solution.py:445
  29.8 0.9 all-to-all-done.1
  30.7 8.1 %all-to-all-start = ((bf16[32,144,128]{2,1,0:T(8,128)(2,1)}), bf16[32,144,128]{2,1,0:T(8,128)(2,1)S(1)}, u32[]{:S(2)}, u32[]{:S(2)}) async-start(bf16[32,144,128]{2,1,0:T(8,128)(2,1)} %reshape.35), calls=%async_computation | async-start | bytes 2359296 | tf_op jit(solution)/shard_map/all_to_all | solution.py:447
  38.8 0.7 slice_reduce_fusion
  39.5 0.1 reshape_reshape_squeeze.3.refs_1_
  39.6 0.8 copy.53
  40.4 2.7 %reshape.37 = bf16[3,64,36,36]{3,2,1,0:T(8,128)(2,1)S(1)} reshape(bf16[3,8,8,1296]{3,2,1,0:T(8,128)(2,1)} %copy.53) | data formatting | bytes 995328 | tf_op jit(solution)/shard_map/reshape | solution.py:455
  43.1 0.5 fusion.11
  43.6 0.4 pad_maximum_fusion.2.refs_2_
  44.0 3.8 %pad_maximum_fusion = (bf16[64,48,144]{2,1,0:T(8,128)(2,1)}, bf16[64,48,144]{2,1,0:T(8,128)(2,1)}) fusion(bf16[64,48,48]{2,1,0:T(8,128)(2,1)S(1)} %get-tuple-element.15, bf16[64,48,48]{2,1,0:T(8,128)(2,1)S(1)} %get-tuple-element.14), kind=kLoop, calls=%fused_computation.9 | loop fusion | flops 5308416 | bytes 2359296 | tf_op jit(solution)/shard_map/concatenate | solution.py:459
  47.9 20.3 %all-to-all-done = bf16[32,144,128]{2,1,0:T(8,128)(2,1)S(1)} async-done(((bf16[32,144,128]{2,1,0:T(8,128)(2,1)}), bf16[32,144,128]{2,1,0:T(8,128)(2,1)S(1)}, u32[]{:S(2)}, u32[]{:S(2)}) %all-to-all-start) | async-done | bytes 1179680 | tf_op jit(solution)/shard_map/all_to_all | solution.py:447
  68.1 0.0 copy-start
  68.1 1.0 copy-done
  69.2 0.0 copy-start.1
  69.2 1.0 copy-done.1
  70.2 0.0 copy-start.2
  70.2 1.0 copy-done.2
  71.2 1.0 copy-done.3
  72.3 52.8 %shard_map.123 = bf16[32,144,128]{2,1,0:T(8,128)(2,1)S(1)} custom-call(bf16[4,8,144,128]{3,2,1,0:T(8,128)(2,1)S(1)} %bitcast.43, f32[1,256]{1,0:T(1,128)S(1)} %reshape_reshape_squeeze.3.refs_1_, bf16[64,48,96]{2,1,0:T(8,128)(2,1)S(1)} %pad_maximum_fusion.2.refs_2_, bf16[64,48,144]{2,1,0:T(8,128)(2,1)} %get-tuple-element.17.refs_3_, ...), custom_call_target="tpu_custom_call" | custom-call | tf_op jit(solution)/shard_map/pallas_call | solution.py:463
  125.1 1.1 reshape.38
  126.2 0.0 copy-start.7
  126.2 0.9 copy.54
  127.1 0.0 copy-done.7
  127.1 0.7 convolution_bitcast_fusion.1
  127.9 0.4 fusion.22
  128.3 0.8 copy.56
  129.0 2.0 %copy.58 = bf16[64,8,576]{2,1,0:T(8,128)(2,1)} copy(bf16[64,8,576]{0,1,2:T(8,128)(2,1)S(1)} %bitcast.47) | data formatting | bytes 1179648
  131.1 0.8 copy.55
  131.8 2.0 %copy.57 = bf16[64,8,576]{2,1,0:T(8,128)(2,1)} copy(bf16[64,8,576]{0,1,2:T(8,128)(2,1)S(1)} %bitcast.48) | data formatting | bytes 1179648
  (1 shorter events, 0.0 us)
Async XLA Ops:
  13.8 5.6 %copy-start.4 = (bf16[64,8,576]{2,1,0:T(8,128)(2,1)S(1)}, bf16[64,8,576]{2,1,0:T(8,128)(2,1)}, u32[]{:S(2)}) copy-start(bf16[64,8,576]{2,1,0:T(8,128)(2,1)} %param.11) | copy-start | bytes 1769476
  14.7 16.0 %all-to-all-start.1 = ((bf16[8,3,8,1296]{3,2,1,0:T(8,128)(2,1)}), bf16[8,3,8,1296]{3,2,1,0:T(8,128)(2,1)S(1)}, u32[]{:S(2)}, u32[]{:S(2)}) async-start(bf16[8,3,8,1296]{3,2,1,0:T(8,128)(2,1)} %copy.52), calls=%async_computation.1 | async-start | bytes 1081344 | tf_op jit(solution)/shard_map/all_to_all | solution.py:454
  20.8 1.1 copy-start.5
  23.3 0.8 copy-start.6
  30.7 37.4 %all-to-all-start = ((bf16[32,144,128]{2,1,0:T(8,128)(2,1)}), bf16[32,144,128]{2,1,0:T(8,128)(2,1)S(1)}, u32[]{:S(2)}, u32[]{:S(2)}) async-start(bf16[32,144,128]{2,1,0:T(8,128)(2,1)} %reshape.35), calls=%async_computation | async-start | bytes 2359296 | tf_op jit(solution)/shard_map/all_to_all | solution.py:447
  68.1 1.0 copy-start
  69.2 1.0 copy-start.1
  70.2 1.0 copy-start.2
  71.2 1.0 copy-start.3
  126.2 0.9 copy-start.7

commit v3 on v2

--- a/solution.py
+++ b/solution.py
@@ -289,13 +289,25 @@
 
 def chain_kernel(
     shares, strips, half_cols,
-    recv_ref, sigma_ref, inv_ref, west_ref, east_ref,
+    source_ref, sigma_ref, flat_ref, fhi_in, flo_in, bhi_in, blo_in,
+    out_ref,
+    x_ref, a_ref, b_ref, inv_ref, square_ref, recv_ref, planes_ref,
     fhi_ref, flo_ref, bhi_ref, blo_ref,
-    out_ref, x_ref, a_ref, b_ref, planes_ref, send_sems, recv_sems, own_sem,
+    first_send, first_recv, send_sems, recv_sems, own_sem, table_sems,
 ):
     my_share, my_strip = lax.axis_index("plane"), lax.axis_index("strip")
     me = my_share * strips + my_strip
     devices = shares * strips
+    tables = [
+        pltpu.make_async_copy(given, kept, table_sems.at[place])
+        for place, (given, kept) in enumerate(
+            [(fhi_in, fhi_ref), (flo_in, flo_ref), (bhi_in, bhi_ref), (blo_in, blo_ref)]
+        )
+    ]
+    own_source = pltpu.make_async_copy(source_ref.at[me], recv_ref.at[me], own_sem)
+    own_source.start()
+    for table in tables:
+        table.start()
 
     barrier = pltpu.get_barrier_semaphore()
 
@@ -307,6 +319,23 @@
         return carry
 
     lax.fori_loop(1, devices, greet, 0)
+
+    pl.semaphore_wait(barrier, devices - 1)
+
+    def source_copy(other, slot):
+        return pltpu.make_async_remote_copy(
+            src_ref=source_ref.at[other],
+            dst_ref=recv_ref.at[slot],
+            send_sem=first_send.at[other],
+            recv_sem=first_recv.at[slot],
+            device_id={"plane": other // strips, "strip": other % strips},
+        )
+
+    def send_source(step, carry):
+        source_copy((me + step) % devices, me).start()
+        return carry
+
+    lax.fori_loop(1, devices, send_source, 0)
 
     def result_copy(share, strip, slot):
         return pltpu.make_async_remote_copy(
@@ -319,18 +348,41 @@
 
     columns = x_ref.shape[0]
     modes = x_ref.shape[2]
+    per_strip = 2 * half_cols
+    square_ref[...] = jnp.zeros_like(square_ref)
+
+    def unflatten(strip, carry):
+        flat = flat_ref[strip].astype(jnp.float32)
+        for row in range(NODES):
+            square_ref[strip, :, row, :NODES] = flat[:, row * NODES : (row + 1) * NODES]
+        return carry
+
+    lax.fori_loop(0, strips, unflatten, 0)
+
+    def repeated(count):
+        row = lax.broadcasted_iota(jnp.int32, (PAD, count * PAD), 0)
+        lane = lax.broadcasted_iota(jnp.int32, (PAD, count * PAD), 1)
+        return (row == lane % PAD).astype(jnp.bfloat16)
+
     lane = lax.broadcasted_iota(jnp.int32, (PAD, 3 * PAD), 1)
+    twice, thrice = repeated(2), repeated(3)
+
+    def block(kind, column):
+        strip, place = column // per_strip, column % per_strip
+        return square_ref[strip, kind * per_strip + place][:, :PAD].astype(jnp.bfloat16)
 
     def folded(left, right):
+        right = dot(right, thrice).astype(jnp.bfloat16)
         high, low = split(dot(left, right))
         return jnp.where(lane < 2 * PAD, high.astype(jnp.float32), low.astype(jnp.float32)).astype(
             jnp.bfloat16
         )
 
     def prepare(column, carry):
-        inverse = inv_ref[column][:, :PAD]
-        a_ref[column] = folded(inverse, west_ref[column])
-        b_ref[column] = folded(inverse, east_ref[jnp.minimum(column + 1, columns - 1)])
+        inverse = block(0, column)
+        inv_ref[column] = dot(inverse, twice).astype(jnp.bfloat16)
+        a_ref[column] = folded(inverse, block(1, column))
+        b_ref[column] = folded(inverse, block(2, jnp.minimum(column + 1, columns - 1)))
         return carry
 
     lax.fori_loop(0, columns, prepare, 0, unroll=4)
@@ -342,7 +394,15 @@
         return jnp.concatenate([high, low, high], axis=0)
 
     def forward(strip, previous):
-        planes = jnp.concatenate([recv_ref[share, strip] for share in range(shares)], axis=1)
+        for share in range(shares):
+
+            @pl.when(share * strips + strip != me)
+            def _():
+                source_copy(me, share * strips + strip).wait_recv()
+
+        planes = jnp.concatenate(
+            [recv_ref[share * strips + strip] for share in range(shares)], axis=1
+        )
         coeffs = dot(planes, fhi_ref[...]) + dot(planes, flo_ref[...])
         sources = []
         for half in range(2):
@@ -359,8 +419,10 @@
         return previous
 
     nothing = jnp.zeros((PAD, modes), jnp.float32)
+    own_source.wait()
+    for table in tables:
+        table.wait()
     lax.fori_loop(0, strips, forward, nothing)
-    pl.semaphore_wait(barrier, devices - 1)
 
     def backward(step, following):
         strip = strips - 1 - step
@@ -398,6 +460,7 @@
         source = (me + step) % devices
         result_copy(source // strips, source % strips, source).wait_recv()
         result_copy(source // strips, source % strips, me).wait_send()
+        source_copy(source, me).wait_send()
         return carry
 
     lax.fori_loop(1, devices, finish, 0)
@@ -444,40 +507,38 @@
         .transpose(2, 4, 3, 1, 6, 0, 5)
         .reshape(shares * strips, half_cols * NODES, 2 * planes_dev)
     )
-    received = lax.all_to_all(outgoing, ("plane", "strip"), 0, 0, tiled=True)
-    received = received.reshape(shares, strips, half_cols * NODES, 2 * planes_dev)
-
     group = lax.axis_index("plane") // 2
     own = lax.dynamic_slice_in_dim(labels, group * strips, strips, 2)
     matrices = jnp.stack([dinv, west_coupling, east_coupling])
     matrices = jnp.einsum("grc,mgre->cmge", own, matrices)
     matrices = lax.all_to_all(matrices, "strip", 0, 0, tiled=True)
-    matrices = matrices.transpose(1, 0, 2, 3).reshape(3, all_columns, NODES, NODES)
-    spare = PAD - NODES
-    matrices = jnp.pad(matrices, ((0, 0), (0, 0), (0, spare), (0, spare)))
-    inverse = jnp.concatenate([matrices[0]] * 2, axis=2)
-    from_west = jnp.concatenate([matrices[1]] * 3, axis=2)
-    from_east = jnp.concatenate([matrices[2]] * 3, axis=2)
+    matrices = matrices.reshape(strips, 3 * columns, NODES * NODES)
 
     (fhi, flo), (bhi, blo) = transform_tables(planes, shares)
     result = pl.pallas_call(
         lambda *refs: chain_kernel(shares, strips, half_cols, *refs),
         out_shape=jax.ShapeDtypeStruct(outgoing.shape, jnp.bfloat16),
-        in_specs=[vmem] * 9,
+        in_specs=[vmem] * 3 + [pl.BlockSpec(memory_space=pltpu.HBM)] * 4,
         out_specs=vmem,
         scratch_shapes=[
             pltpu.VMEM((all_columns, PAD, planes), jnp.float32),
             pltpu.VMEM((all_columns, PAD, 3 * PAD), jnp.bfloat16),
             pltpu.VMEM((all_columns, PAD, 3 * PAD), jnp.bfloat16),
+            pltpu.VMEM((all_columns, PAD, 2 * PAD), jnp.bfloat16),
+            pltpu.VMEM((strips, 3 * columns, PAD, 128), jnp.float32),
             pltpu.VMEM(outgoing.shape, jnp.bfloat16),
-            pltpu.SemaphoreType.DMA((shares * strips,)),
-            pltpu.SemaphoreType.DMA((shares * strips,)),
+            pltpu.VMEM(outgoing.shape, jnp.bfloat16),
+        ]
+        + [pltpu.VMEM(table.shape, jnp.bfloat16) for table in (fhi, flo, bhi, blo)]
+        + [pltpu.SemaphoreType.DMA((shares * strips,)) for _ in range(4)]
+        + [
             pltpu.SemaphoreType.DMA,
+            pltpu.SemaphoreType.DMA((4,)),
         ],
         compiler_params=pltpu.CompilerParams(
             vmem_limit_bytes=48 * 1024 * 1024, collective_id=1, has_side_effects=True
         ),
-    )(received, sigma_all.reshape(1, planes), inverse, from_west, from_east, fhi, flo, bhi, blo)
+    )(outgoing, sigma_all.reshape(1, planes), matrices, fhi, flo, bhi, blo)
 
     returned = result.reshape(groups, 2, strips, half_cols, NODES, 2, planes_dev)
     returned = returned.transpose(5, 3, 0, 2, 1, 6, 4).reshape(

time: 135 us -> 131 us (0.970)
  Pallas kernels: 61.6 us -> 89.5 us
  waiting for transfers between devices: 21.1 us -> 0.01 us
  starting transfers between devices: 12.8 us -> 4.7 us
  other arithmetic: 5.63 us -> 1.39 us
  local copies, waits for them, and re-layouts: 28.4 us -> 30 us
    pallas_call x1, Pallas kernels: 52.8 us -> 80.8 us  [chain_on_device(): pl.pallas_call(lambda *refs: chain_kernel(shares, strips, half_cols, *ref...]
    all_to_all x1 -> x0, waiting for transfers between devices: 20.3 us -> none  [chain_on_device(): received = lax.all_to_all(outgoing, ('plane', 'strip'), 0, 0, tiled=True)]
    all_to_all x1 -> x0, starting transfers between devices: 8.09 us -> none  [chain_on_device(): received = lax.all_to_all(outgoing, ('plane', 'strip'), 0, 0, tiled=True)]
    concatenate x2 -> x0, other arithmetic: 4.25 us -> none  [the longest x1 3.81 us: chain_on_device(): from_west = jnp.concatenate([matrices[1]] * 3, axis=2)]
    transpose x2 -> x0, local copies, waits for them, and re-layouts: 3.27 us -> none  [the longest x1 2.43 us: chain_on_device(): outgoing = outgoing.reshape(2, half_cols, groups, strips, 2, planes_dev,...]
    reshape x1, local copies, waits for them, and re-layouts: 2.23 us -> 4.32 us  [chain_on_device(): outgoing = outgoing.reshape(2, half_cols, groups, strips, 2, planes_dev,...]
    transpose x1, local copies, waits for them, and re-layouts: 0.91 us -> 2.58 us  [chain_on_device(): returned.transpose(5, 3, 0, 2, 1, 6, 4)]
    reshape x1, local copies, waits for them, and re-layouts: 1.06 us -> 2.49 us  [chain_on_device(): result.reshape(groups, 2, strips, half_cols, NODES, 2, planes_dev)]
  transfers between devices with their start and end apart: 2 -> 1, of which waited for: 2 -> 0; matrix products, arithmetic and copies ran while one was open for 14% -> 11% of each run, Pallas kernels for 0% -> 0%
where the time goes in v3:
time: 131 us; the launch traced here: 130 us
  Pallas kernels  89.5 us (68%)
  local copies, waits for them, and re-layouts  30 us (23%)
  starting transfers between devices  4.7 us (4%)
  matrix products  3.52 us (3%)
  other arithmetic  1.39 us (1%)
    pallas_call x1, Pallas kernels, chain_on_device(): pl.pallas_call(lambda *refs: chain_kernel(shares, strips, half_cols, *ref...  80.8 us
    unnamed x18, local copies, waits for them, and re-layouts  10.9 us
    pallas_call x1, Pallas kernels, chain_on_device(): pl.pallas_call(label_kernel, out_shape=(jax.ShapeDtypeStruct((columns, ro...  8.76 us
    all_to_all x1, starting transfers between devices, chain_on_device(): matrices = lax.all_to_all(matrices, 'strip', 0, 0, tiled=True)  4.7 us
    reshape x1, local copies, waits for them, and re-layouts, chain_on_device(): outgoing = outgoing.reshape(2, half_cols, groups, strips, 2, planes_dev,...  4.32 us
    reshape x1, local copies, waits for them, and re-layouts, chain_on_device(): outgoing.reshape(2, half_cols, groups, strips, 2, planes_dev, NODES)  3.84 us
  transfers between devices with their start and end apart: 1, of which 0 were waited for; matrix products, arithmetic and copies ran while one was open for 11% of the time, Pallas kernels for 0%

profile of v3, /device:TPU:5, one launch (start us, length us, event | category | flops | bytes accessed | tf_op | source)
XLA Modules:
  0.0 129.9 jit_solution(12536825698215072347)
XLA Ops:
  0.6 1.4 %fusion.9.onehot_ref = bf16[8,16,16]{2,1,0:T(8,128)(2,1)} fusion(s32[8,16]{1,0:T(8,128)} %param.14), kind=kLoop, calls=%fused_computation.13 | loop fusion | flops 4096 | bytes 4608 | tf_op jit(solution)/shard_map/convert_element_type | solution.py:479
  2.0 0.7 pad.4
  2.7 0.6 broadcast_in_dim.2.sigma_ref
  3.3 8.8 %shard_map.122 = (bf16[8,16,128]{2,1,0:T(8,128)(2,1)}, f32[4,8,128]{2,1,0:T(8,128)}) custom-call(bf16[8,16,16]{2,1,0:T(8,128)(2,1)} %fusion.9.onehot_ref, f32[8,128]{1,0:T(8,128)} %broadcast_in_dim.2.sigma_ref), custom_call_target="tpu_custom_call" | custom-call | tf_op jit(solution)/shard_map/pallas_call | solution.py:481
  12.0 1.7 %convolution_bitcast_fusion = bf16[8,3,8,1296]{3,0,1,2:T(8,128)(2,1)S(1)} fusion(bf16[1,8,16,1296]{3,2,0,1:T(8,128)(2,1)} %bitcast.45, bf16[1,8,16,1296]{3,2,0,1:T(8,128)(2,1)} %bitcast.46, bf16[1,8,16,1296]{3,2,0,1:T(8,128)(2,1)} %bitcast.47, bf16[8,16,16]{2,1,0:T(8,128)(2,1)} %bitcast.44, s32[]{:T(128)S(6)} %select_n.9), kind=kOutput, calls=%fused_computation | convolution fusion | flops 8957952 | bytes 1497092 | tf_op jit(solution)/shard_map/grc,mgre->cmge/dot_general | solution.py:513
  13.8 0.0 copy-start.4
  13.8 0.9 copy.52
  14.6 4.7 %all-to-all-start = ((bf16[8,3,8,1296]{3,2,1,0:T(8,128)(2,1)}), bf16[8,3,8,1296]{3,2,1,0:T(8,128)(2,1)S(1)}, u32[]{:S(2)}, u32[]{:S(2)}) async-start(bf16[8,3,8,1296]{3,2,1,0:T(8,128)(2,1)} %copy.52), calls=%async_computation | async-start | bytes 1081344 | tf_op jit(solution)/shard_map/all_to_all | solution.py:514
  19.3 0.0 copy-done.4
  19.3 1.4 %copy.46 = bf16[64,8,576]{0,1,2:T(8,128)(2,1)S(1)} copy(bf16[64,8,576]{2,1,0:T(8,128)(2,1)S(1)} %copy-done.4) | data formatting | bytes 1179648 | tf_op args[1]
  20.8 0.0 copy-start.5
  20.8 0.5 copy.48
  21.3 0.6 copy-done.5
  21.9 1.4 %copy.45 = bf16[64,8,576]{0,1,2:T(8,128)(2,1)S(1)} copy(bf16[64,8,576]{2,1,0:T(8,128)(2,1)S(1)} %copy-done.5) | data formatting | bytes 1179648 | tf_op args[0]
  23.3 0.0 copy-start.6
  23.3 0.5 copy.47
  23.8 0.3 copy-done.6
  24.1 1.1 fusion
  25.1 3.8 %copy.66 = bf16[2,4,2,8,2,64,36]{5,0,6,1,3,4,2:T(2,128)(2,1)} copy(bf16[2,4,2,8,2,64,36]{5,3,2,6,4,1,0:T(8,128)(2,1)S(1)} %bitcast.36) | data formatting | bytes 2359296 | tf_op jit(solution)/shard_map/reshape | solution.py:506
  29.0 0.0 copy-start
  29.0 4.3 %reshape.32.refs_0_ = bf16[32,144,128]{2,1,0:T(8,128)(2,1)S(1)} reshape(bf16[2,2,8,4,36,2,64]{6,5,4,3,2,1,0:T(2,128)(2,1)} %bitcast.38) | data formatting | bytes 2359296 | tf_op jit(solution)/shard_map/reshape | solution.py:508
  33.3 0.7 slice_reduce_fusion
  34.0 0.1 reshape_reshape_squeeze.3.refs_1_
  34.1 0.0 all-to-all-done
  34.1 0.0 copy-done
  34.1 0.0 copy-start.1
  34.1 1.0 copy-done.1
  35.2 0.0 copy-start.2
  35.2 1.0 copy-done.2
  36.2 0.0 copy-start.3
  36.2 1.0 copy-done.3
  37.3 80.8 %shard_map.123 = bf16[32,144,128]{2,1,0:T(8,128)(2,1)S(1)} custom-call(bf16[32,144,128]{2,1,0:T(8,128)(2,1)S(1)} %reshape.32.refs_0_, f32[1,256]{1,0:T(1,128)S(1)} %reshape_reshape_squeeze.3.refs_1_, bf16[8,24,1296]{2,1,0:T(8,128)(2,1)S(1)} %bitcast.35, bf16[512,512]{1,0:T(8,128)(2,1)S(1)} %copy-done, bf16[512,512]{1,0:T(8,128)(2,1)S(1)} %copy-done.1, ...), custom_call_target="tpu_custom_call" | custom-call | tf_op jit(solution)/shard_map/pallas_call | solution.py:518
  118.0 2.5 %reshape.34 = bf16[2,2,8,4,36,2,64]{6,5,4,3,2,1,0:T(2,128)(2,1)} reshape(bf16[32,144,128]{2,1,0:T(8,128)(2,1)S(1)} %shard_map.123) | data formatting | bytes 2359296 | tf_op jit(solution)/shard_map/reshape | solution.py:543
  120.5 2.6 %copy.53 = bf16[2,4,2,8,2,64,36]{5,3,2,6,4,1,0:T(8,128)(2,1)S(1)} copy(bf16[2,4,2,8,2,64,36]{5,0,6,1,3,4,2:T(2,128)(2,1)} %bitcast.39) | data formatting | bytes 2359296 | tf_op jit(solution)/shard_map/transpose | solution.py:544
  123.1 0.7 convolution_bitcast_fusion.1
  123.8 0.4 fusion.19
  124.3 0.8 copy.54
  125.0 2.0 %copy.56 = bf16[64,8,576]{2,1,0:T(8,128)(2,1)} copy(bf16[64,8,576]{0,1,2:T(8,128)(2,1)S(1)} %bitcast.40) | data formatting | bytes 1179648
  127.1 0.8 copy.55
  127.8 2.0 %copy.57 = bf16[64,8,576]{2,1,0:T(8,128)(2,1)} copy(bf16[64,8,576]{0,1,2:T(8,128)(2,1)S(1)} %bitcast.41) | data formatting | bytes 1179648
Async XLA Ops:
  13.8 5.6 %copy-start.4 = (bf16[64,8,576]{2,1,0:T(8,128)(2,1)S(1)}, bf16[64,8,576]{2,1,0:T(8,128)(2,1)}, u32[]{:S(2)}) copy-start(bf16[64,8,576]{2,1,0:T(8,128)(2,1)} %param.12) | copy-start | bytes 1769476
  14.6 19.5 %all-to-all-start = ((bf16[8,3,8,1296]{3,2,1,0:T(8,128)(2,1)}), bf16[8,3,8,1296]{3,2,1,0:T(8,128)(2,1)S(1)}, u32[]{:S(2)}, u32[]{:S(2)}) async-start(bf16[8,3,8,1296]{3,2,1,0:T(8,128)(2,1)} %copy.52), calls=%async_computation | async-start | bytes 1081344 | tf_op jit(solution)/shard_map/all_to_all | solution.py:514
  20.8 1.1 copy-start.5
  23.3 0.8 copy-start.6
  29.0 5.2 %copy-start = (bf16[512,512]{1,0:T(8,128)(2,1)S(1)}, bf16[512,512]{1,0:T(8,128)(2,1)}, u32[]{:S(2)}) copy-start(bf16[512,512]{1,0:T(8,128)(2,1)} %constant.34.clone.refs_3_) | copy-start | bytes 1572868
  34.1 1.0 copy-start.1
  35.2 1.0 copy-start.2
  36.2 1.0 copy-start.3

commit v4 on v3

--- a/solution.py
+++ b/solution.py
@@ -287,6 +287,67 @@
         plane_copy(step, my_share).wait_send()
 
 
+def pack_kernel(strips, rows_ref, u_ref, v_ref, out_ref, wide_ref, turned_ref):
+    planes_dev, columns, flat_width = u_ref.shape
+    rows, half_cols = flat_width // NODES, columns // 2
+    for field, given in enumerate((u_ref, v_ref)):
+        wide_ref[...] = given[...].astype(jnp.float32)
+        for place in range(half_cols):
+            both = jnp.concatenate([wide_ref[:, place, :], wide_ref[:, half_cols + place, :]], 0)
+            turned = both.T
+            for row in range(rows):
+                turned_ref[field, place, row, :NODES] = turned[row * NODES : (row + 1) * NODES]
+    first = lax.broadcasted_iota(jnp.int32, (NODES, 2 * planes_dev), 1) < planes_dev
+
+    def emit(chain, carry):
+        for field in range(2):
+            pieces = [
+                jnp.where(
+                    first,
+                    turned_ref[field, place, rows_ref[place, chain], :NODES],
+                    turned_ref[field, place, rows_ref[half_cols + place, chain], :NODES],
+                )
+                for place in range(half_cols)
+            ]
+            device = (chain // strips * 2 + field) * strips + chain % strips
+            out_ref[device] = jnp.concatenate(pieces, axis=0).astype(jnp.bfloat16)
+        return carry
+
+    lax.fori_loop(0, rows, emit, 0)
+
+
+def unpack_kernel(strips, chains_ref, given_ref, u_ref, v_ref, wide_ref, turned_ref):
+    planes_dev, columns, flat_width = u_ref.shape
+    rows, half_cols = flat_width // NODES, columns // 2
+
+    def take(chain, carry):
+        for field in range(2):
+            device = (chain // strips * 2 + field) * strips + chain % strips
+            given = given_ref[device].astype(jnp.float32)
+            for place in range(half_cols):
+                turned_ref[field, place, chain, :NODES] = given[
+                    place * NODES : (place + 1) * NODES
+                ]
+        return carry
+
+    lax.fori_loop(0, rows, take, 0)
+    first = lax.broadcasted_iota(jnp.int32, (NODES, 2 * planes_dev), 1) < planes_dev
+    for field, out_ref in enumerate((u_ref, v_ref)):
+        for place in range(half_cols):
+            pieces = [
+                jnp.where(
+                    first,
+                    turned_ref[field, place, chains_ref[place, row], :NODES],
+                    turned_ref[field, place, chains_ref[half_cols + place, row], :NODES],
+                )
+                for row in range(rows)
+            ]
+            both = jnp.concatenate(pieces, axis=0).T
+            wide_ref[:, place, :] = both[:planes_dev]
+            wide_ref[:, half_cols + place, :] = both[planes_dev:]
+        out_ref[...] = wide_ref[...].astype(jnp.bfloat16)
+
+
 def chain_kernel(
     shares, strips, half_cols,
     source_ref, sigma_ref, flat_ref, fhi_in, flo_in, bhi_in, blo_in,
@@ -393,7 +454,8 @@
         high, low = split(value)
         return jnp.concatenate([high, low, high], axis=0)
 
-    def forward(strip, previous):
+    def to_modes(step, carry):
+        strip = (my_strip + strips - step) % strips
         for share in range(shares):
 
             @pl.when(share * strips + strip != me)
@@ -404,54 +466,76 @@
             [recv_ref[share * strips + strip] for share in range(shares)], axis=1
         )
         coeffs = dot(planes, fhi_ref[...]) + dot(planes, flo_ref[...])
-        sources = []
         for half in range(2):
             for place in range(half_cols):
                 own = coeffs[place * NODES : (place + 1) * NODES, half * modes : (half + 1) * modes]
                 own = jnp.concatenate([own, jnp.zeros((PAD - NODES, modes), jnp.float32)], axis=0)
                 high, low = split(own)
                 column = (strip * 2 + half) * half_cols + place
-                sources.append(dot(inv_ref[column], jnp.concatenate([high, low], axis=0)))
-        for place in range(2 * half_cols):
-            column = strip * 2 * half_cols + place
-            previous = sources[place] - sigma * dot(a_ref[column], stacked(previous))
-            x_ref[column] = previous
-        return previous
-
-    nothing = jnp.zeros((PAD, modes), jnp.float32)
+                x_ref[column] = dot(inv_ref[column], jnp.concatenate([high, low], axis=0))
+        return carry
+
     own_source.wait()
     for table in tables:
         table.wait()
+    lax.fori_loop(0, strips, to_modes, 0)
+
+    def forward(strip, previous):
+        for place in range(per_strip):
+            column = strip * per_strip + place
+            previous = x_ref[column] - sigma * dot(a_ref[column], stacked(previous))
+            x_ref[column] = previous
+        return previous
+
+    nothing = jnp.zeros((PAD, modes), jnp.float32)
     lax.fori_loop(0, strips, forward, nothing)
 
-    def backward(step, following):
-        strip = strips - 1 - step
-        solved = [None] * (2 * half_cols)
-        for place in reversed(range(2 * half_cols)):
-            column = strip * 2 * half_cols + place
-            following = x_ref[column] - sigma * dot(b_ref[column], stacked(following))
+    def solve(strip, following):
+        solved = [x_ref[strip * per_strip + place] for place in range(per_strip)]
+        for place in reversed(range(per_strip)):
+            factors = b_ref[strip * per_strip + place]
+            following = solved[place] - sigma * dot(factors, stacked(following))
             solved[place] = following
-        pieces = [
-            jnp.concatenate([solved[place][:NODES], solved[half_cols + place][:NODES]], axis=1)
-            for place in range(half_cols)
-        ]
+        return solved
+
+    def keep(strip, solved):
+        for place in range(per_strip):
+            x_ref[strip * per_strip + place] = solved[place]
+
+    def planes_of(strip):
+        pieces = []
+        for place in range(half_cols):
+            first = x_ref[strip * per_strip + place]
+            second = x_ref[strip * per_strip + half_cols + place]
+            pieces.append(jnp.concatenate([first[:NODES], second[:NODES]], axis=1))
         high, low = split(jnp.concatenate(pieces, axis=0))
-        planes = dot(high, bhi_ref[...]) + dot(low, bhi_ref[...]) + dot(high, blo_ref[...])
+        return dot(high, bhi_ref[...]) + dot(low, bhi_ref[...]) + dot(high, blo_ref[...])
+
+    def send(strip, planes):
         width = planes.shape[1] // shares
         for share in range(shares):
             planes_ref[share * strips + strip] = planes[
                 :, share * width : (share + 1) * width
             ].astype(jnp.bfloat16)
         for share in range(shares):
-            mine = (share == my_share) & (strip == my_strip)
-
-            @pl.when(jnp.logical_not(mine))
+
+            @pl.when(share * strips + strip != me)
             def _():
                 result_copy(share, strip, me).start()
 
-        return following
-
-    lax.fori_loop(0, strips, backward, nothing)
+    last = solve(strips - 1, nothing)
+    keep(strips - 1, last)
+
+    def backward(step, following):
+        strip = strips - 1 - step
+        planes = planes_of(strip + 1)
+        solved = solve(strip, following)
+        keep(strip, solved)
+        send(strip + 1, planes)
+        return solved[0]
+
+    lax.fori_loop(1, strips, backward, last[0])
+    send(0, planes_of(0))
     own_copy = pltpu.make_async_copy(planes_ref.at[me], out_ref.at[me], own_sem)
     own_copy.start()
     own_copy.wait()
@@ -500,13 +584,26 @@
     labels = labels[:, :, :rows]
     sigma_all = sigma_tiles[:, 0, :planes_dev].reshape(planes)
 
-    fields = jnp.stack([u_field, v_field]).reshape(2, planes_dev, columns, rows, NODES)
-    outgoing = jnp.einsum("grc,fzgrn->gcfzn", labels, fields)
-    outgoing = (
-        outgoing.reshape(2, half_cols, groups, strips, 2, planes_dev, NODES)
-        .transpose(2, 4, 3, 1, 6, 0, 5)
-        .reshape(shares * strips, half_cols * NODES, 2 * planes_dev)
-    )
+    row_ids = jnp.arange(rows, dtype=jnp.int32)
+    whole = labels.astype(jnp.int32)
+    rows_of = jnp.sum(whole * row_ids[None, :, None], axis=1)
+    chains_of = jnp.sum(whole * row_ids[None, None, :], axis=2)
+    smem = pl.BlockSpec(memory_space=pltpu.SMEM)
+    spare_space = [
+        pltpu.VMEM((planes_dev, columns, flat_width), jnp.float32),
+        pltpu.VMEM((2, half_cols, rows, 40, 2 * planes_dev), jnp.float32),
+    ]
+    outgoing = pl.pallas_call(
+        lambda *refs: pack_kernel(strips, *refs),
+        out_shape=jax.ShapeDtypeStruct(
+            (shares * strips, half_cols * NODES, 2 * planes_dev), jnp.bfloat16
+        ),
+        in_specs=[smem, vmem, vmem],
+        out_specs=vmem,
+        scratch_shapes=spare_space,
+        compiler_params=pltpu.CompilerParams(vmem_limit_bytes=32 * 1024 * 1024),
+    )(rows_of, u_field, v_field)
+
     group = lax.axis_index("plane") // 2
     own = lax.dynamic_slice_in_dim(labels, group * strips, strips, 2)
     matrices = jnp.stack([dinv, west_coupling, east_coupling])
@@ -540,14 +637,17 @@
         ),
     )(outgoing, sigma_all.reshape(1, planes), matrices, fhi, flo, bhi, blo)
 
-    returned = result.reshape(groups, 2, strips, half_cols, NODES, 2, planes_dev)
-    returned = returned.transpose(5, 3, 0, 2, 1, 6, 4).reshape(
-        columns, rows, 2, planes_dev, NODES
-    )
-    outs = jnp.einsum("grc,gcfzn->fzgrn", labels, returned).reshape(
-        2, planes_dev, columns, flat_width
-    )
-    return outs[0], outs[1]
+    return pl.pallas_call(
+        lambda *refs: unpack_kernel(strips, *refs),
+        out_shape=(
+            jax.ShapeDtypeStruct(u_field.shape, jnp.bfloat16),
+            jax.ShapeDtypeStruct(v_field.shape, jnp.bfloat16),
+        ),
+        in_specs=[smem, vmem],
+        out_specs=(vmem, vmem),
+        scratch_shapes=spare_space,
+        compiler_params=pltpu.CompilerParams(vmem_limit_bytes=32 * 1024 * 1024),
+    )(chains_of, result)
 
 
 def solution(mesh):

time: 131 us -> 123 us (0.939)
  local copies, waits for them, and re-layouts: 30 us -> 7.35 us
  Pallas kernels: 89.5 us -> 98.9 us
  waiting for transfers between devices: 0.01 us -> 6.57 us
  matrix products: 3.52 us -> 1.71 us
    reshape x3 -> x0, local copies, waits for them, and re-layouts: 10.6 us -> none  [the longest x1 4.32 us: chain_on_device(): outgoing = outgoing.reshape(2, half_cols, groups, strips, 2, planes_dev,...]
    unnamed x18, local copies, waits for them, and re-layouts: 10.9 us -> 3.83 us
    all_to_all x1, waiting for transfers between devices: 0.01 us -> 6.57 us  [chain_on_device(): matrices = lax.all_to_all(matrices, 'strip', 0, 0, tiled=True)]
    pallas_call x0 -> x2, Pallas kernels: none -> 5.84 us  [the longest x1 3.31 us: chain_on_device(): pl.pallas_call(lambda *refs: unpack_kernel(strips, *refs), out_shape=(jax...]
    pallas_call x1, Pallas kernels: 80.8 us -> 84.3 us  [chain_on_device(): pl.pallas_call(lambda *refs: chain_kernel(shares, strips, half_cols, *ref...]
    transpose x1 -> x0, local copies, waits for them, and re-layouts: 2.58 us -> none  [chain_on_device(): returned.transpose(5, 3, 0, 2, 1, 6, 4)]
    slice x3 -> x0, local copies, waits for them, and re-layouts: 1.94 us -> none  [chain_on_device(): return (outs[0], outs[1])]
    dot_general x2 -> x0, matrix products: 1.81 us -> none  [the longest x1 1.07 us: chain_on_device(): outgoing = jnp.einsum('grc,fzgrn->gcfzn', labels, fields)]
  transfers between devices with their start and end apart: 1 -> 1, of which waited for: 0 -> 1; matrix products, arithmetic and copies ran while one was open for 11% -> 2% of each run, Pallas kernels for 0% -> 2%
where the time goes in v4:
time: 123 us; the launch traced here: 122 us
  Pallas kernels  98.9 us (80%)
  local copies, waits for them, and re-layouts  7.35 us (6%)
  waiting for transfers between devices  6.57 us (5%)
  starting transfers between devices  4.7 us (4%)
  other arithmetic  2.2 us (2%)
  matrix products  1.71 us (1%)
    pallas_call x1, Pallas kernels, chain_on_device(): pl.pallas_call(lambda *refs: chain_kernel(shares, strips, half_cols, *ref...  84.3 us
    pallas_call x1, Pallas kernels, chain_on_device(): pl.pallas_call(label_kernel, out_shape=(jax.ShapeDtypeStruct((columns, ro...  8.76 us
    all_to_all x1, waiting for transfers between devices, chain_on_device(): matrices = lax.all_to_all(matrices, 'strip', 0, 0, tiled=True)  6.57 us
    all_to_all x1, starting transfers between devices, chain_on_device(): matrices = lax.all_to_all(matrices, 'strip', 0, 0, tiled=True)  4.7 us
    unnamed x18, local copies, waits for them, and re-layouts  3.83 us
    pallas_call x1, Pallas kernels, chain_on_device(): pl.pallas_call(lambda *refs: unpack_kernel(strips, *refs), out_shape=(jax...  3.31 us
    pallas_call x1, Pallas kernels, chain_on_device(): pl.pallas_call(lambda *refs: pack_kernel(strips, *refs), out_shape=jax.Sh...  2.53 us
  transfers between devices with their start and end apart: 1, of which 1 were waited for; matrix products, arithmetic and copies ran while one was open for 2% of the time, Pallas kernels for 2%

profile of v4, /device:TPU:5, one launch (start us, length us, event | category | flops | bytes accessed | tf_op | source)
XLA Modules:
  0.0 122.2 jit_solution(1008424135662525689)
XLA Ops:
  0.6 1.4 %fusion.7.onehot_ref = bf16[8,16,16]{2,1,0:T(8,128)(2,1)} fusion(s32[8,16]{1,0:T(8,128)} %param.14), kind=kLoop, calls=%fused_computation.11 | loop fusion | flops 4096 | bytes 4608 | tf_op jit(solution)/shard_map/convert_element_type | solution.py:563
  2.0 0.7 pad.4
  2.7 0.6 broadcast_in_dim.2.sigma_ref
  3.3 8.8 %shard_map.122 = (bf16[8,16,128]{2,1,0:T(8,128)(2,1)}, f32[4,8,128]{2,1,0:T(8,128)}) custom-call(bf16[8,16,16]{2,1,0:T(8,128)(2,1)} %fusion.7.onehot_ref, f32[8,128]{1,0:T(8,128)} %broadcast_in_dim.2.sigma_ref), custom_call_target="tpu_custom_call" | custom-call | tf_op jit(solution)/shard_map/pallas_call | solution.py:565
  12.1 1.7 %convolution_bitcast_fusion = bf16[8,3,8,1296]{3,0,1,2:T(8,128)(2,1)S(1)} fusion(bf16[1,8,16,1296]{3,2,0,1:T(8,128)(2,1)} %bitcast.14, bf16[1,8,16,1296]{3,2,0,1:T(8,128)(2,1)} %bitcast.15, bf16[1,8,16,1296]{3,2,0,1:T(8,128)(2,1)} %bitcast.16, bf16[8,16,16]{2,1,0:T(8,128)(2,1)} %bitcast.13, s32[]{:T(128)S(6)} %select_n.9), kind=kOutput, calls=%fused_computation | convolution fusion | flops 8957952 | bytes 1497092 | tf_op jit(solution)/shard_map/grc,mgre->cmge/dot_general | solution.py:610
  13.8 0.0 copy-start.8
  13.8 0.0 copy-start
  13.8 0.0 copy-start.1
  13.8 0.9 copy.19
  14.7 4.7 %all-to-all-start = ((bf16[8,3,8,1296]{3,2,1,0:T(8,128)(2,1)}), bf16[8,3,8,1296]{3,2,1,0:T(8,128)(2,1)S(1)}, u32[]{:S(2)}, u32[]{:S(2)}) async-start(bf16[8,3,8,1296]{3,2,1,0:T(8,128)(2,1)} %copy.19), calls=%async_computation | async-start | bytes 1081344 | tf_op jit(solution)/shard_map/all_to_all | solution.py:611
  19.4 0.7 slice_reduce_fusion
  20.1 0.7 reshape_reshape_squeeze.3.refs_1_
  20.8 0.0 copy-done.8
  20.8 0.8 fusion.6
  21.6 0.0 copy-done
  21.6 0.0 copy-done.1
  21.6 0.0 copy-start.2
  21.6 2.5 %shard_map.123.refs_0_ = bf16[32,144,128]{2,1,0:T(8,128)(2,1)S(1)} custom-call(s32[8,16]{1,0:T(8,128)S(1)} %get-tuple-element.6.refs_0_, bf16[64,8,576]{2,1,0:T(8,128)(2,1)S(1)} %copy-done, bf16[64,8,576]{2,1,0:T(8,128)(2,1)S(1)} %copy-done.1), custom_call_target="tpu_custom_call" | custom-call | tf_op jit(solution)/shard_map/pallas_call | solution.py:596
  24.1 6.6 %all-to-all-done = bf16[8,3,8,1296]{3,2,1,0:T(8,128)(2,1)S(1)} async-done(((bf16[8,3,8,1296]{3,2,1,0:T(8,128)(2,1)}), bf16[8,3,8,1296]{3,2,1,0:T(8,128)(2,1)S(1)}, u32[]{:S(2)}, u32[]{:S(2)}) %all-to-all-start) | async-done | bytes 497696 | tf_op jit(solution)/shard_map/all_to_all | solution.py:611
  30.7 0.0 copy-done.2
  30.7 0.0 copy-start.3
  30.7 1.0 copy-done.3
  31.7 0.0 copy-start.4
  31.7 1.0 copy-done.4
  32.8 0.0 copy-start.5
  32.8 1.0 copy-done.5
  33.8 0.0 copy-start.7
  33.8 0.7 copy-done.7
  34.5 0.0 copy-start.6
  34.5 84.3 %shard_map.124.refs_1_ = bf16[32,144,128]{2,1,0:T(8,128)(2,1)S(1)} custom-call(bf16[32,144,128]{2,1,0:T(8,128)(2,1)S(1)} %shard_map.123.refs_0_, f32[1,256]{1,0:T(1,128)S(1)} %copy-done.7, bf16[8,24,1296]{2,1,0:T(8,128)(2,1)S(1)} %bitcast.12, bf16[512,512]{1,0:T(8,128)(2,1)S(1)} %copy-done.5, bf16[512,512]{1,0:T(8,128)(2,1)S(1)} %copy-done.4, ...), custom_call_target="tpu_custom_call" | custom-call | tf_op jit(solution)/shard_map/pallas_call | solution.py:615
  118.8 0.0 copy-done.6
  118.9 3.3 %shard_map.125 = (bf16[64,8,576]{2,1,0:T(8,128)(2,1)}, bf16[64,8,576]{2,1,0:T(8,128)(2,1)}) custom-call(s32[8,16]{1,0:T(8,128)S(1)} %copy-done.6, bf16[32,144,128]{2,1,0:T(8,128)(2,1)S(1)} %shard_map.124.refs_1_), custom_call_target="tpu_custom_call" | custom-call | tf_op jit(solution)/shard_map/pallas_call | solution.py:640
Async XLA Ops:
  13.8 7.0 %copy-start.8 = (bf16[8,16,128]{2,1,0:T(8,128)(2,1)S(1)}, bf16[8,16,128]{2,1,0:T(8,128)(2,1)}, u32[]{:S(2)}) copy-start(bf16[8,16,128]{2,1,0:T(8,128)(2,1)} %get-tuple-element.4) | copy-start | bytes 98308
  13.8 7.8 %copy-start = (bf16[64,8,576]{2,1,0:T(8,128)(2,1)S(1)}, bf16[64,8,576]{2,1,0:T(8,128)(2,1)}, u32[]{:S(2)}) copy-start(bf16[64,8,576]{2,1,0:T(8,128)(2,1)} %refs_1_.1) | copy-start | bytes 1769476
  13.8 7.8 %copy-start.1 = (bf16[64,8,576]{2,1,0:T(8,128)(2,1)S(1)}, bf16[64,8,576]{2,1,0:T(8,128)(2,1)}, u32[]{:S(2)}) copy-start(bf16[64,8,576]{2,1,0:T(8,128)(2,1)} %refs_2_.1) | copy-start | bytes 1769476
  14.7 16.0 %all-to-all-start = ((bf16[8,3,8,1296]{3,2,1,0:T(8,128)(2,1)}), bf16[8,3,8,1296]{3,2,1,0:T(8,128)(2,1)S(1)}, u32[]{:S(2)}, u32[]{:S(2)}) async-start(bf16[8,3,8,1296]{3,2,1,0:T(8,128)(2,1)} %copy.19), calls=%async_computation | async-start | bytes 1081344 | tf_op jit(solution)/shard_map/all_to_all | solution.py:611
  21.6 9.1 %copy-start.2 = (bf16[512,512]{1,0:T(8,128)(2,1)S(1)}, bf16[512,512]{1,0:T(8,128)(2,1)}, u32[]{:S(2)}) copy-start(bf16[512,512]{1,0:T(8,128)(2,1)} %constant.37.clone.refs_6_) | copy-start | bytes 1572868
  30.7 1.0 copy-start.3
  31.7 1.0 copy-start.4
  32.8 1.0 copy-start.5
  33.8 0.7 copy-start.7
  34.5 84.3 %copy-start.6 = (s32[8,16]{1,0:T(8,128)S(1)}, s32[8,16]{1,0:T(8,128)}, u32[]{:S(2)}) copy-start(s32[8,16]{1,0:T(8,128)} %get-tuple-element.7.refs_0_) | copy-start | bytes 1540

commit v5 on v4

--- a/solution.py
+++ b/solution.py
@@ -217,8 +217,8 @@
 
 
 def label_kernel(
-    onehot_ref, sigma_ref, labels_ref, sigmas_ref,
-    local_ref, total_ref, totals_ref, strip_send, strip_recv, plane_send, plane_recv,
+    onehot_ref, sigma_in, labels_ref, sigmas_ref,
+    sigma_ref, local_ref, total_ref, totals_ref, strip_send, strip_recv, plane_send, plane_recv,
 ):
     columns, rows, _ = onehot_ref.shape
     shares, strips = sigmas_ref.shape[0], totals_ref.shape[0]
@@ -234,6 +234,8 @@
             barrier, 1, device_id={"plane": (my_share + step) % shares, "strip": my_strip}
         )
 
+    sigma_ref[...] = jnp.zeros_like(sigma_ref)
+    sigma_ref[0:1, : sigma_in.shape[1]] = sigma_in[...]
     start = (
         lax.broadcasted_iota(jnp.int32, (rows, 128), 0)
         == lax.broadcasted_iota(jnp.int32, (rows, 128), 1)
@@ -448,7 +450,10 @@
 
     lax.fori_loop(0, columns, prepare, 0, unroll=4)
 
-    sigma = jnp.broadcast_to(sigma_ref[...], (PAD, modes))
+    sigma = jnp.concatenate(
+        [sigma_ref[share, 0:1, : modes // shares] for share in range(shares)], axis=1
+    )
+    sigma = jnp.broadcast_to(sigma, (PAD, modes))
 
     def stacked(value):
         high, low = split(value)
@@ -561,7 +566,6 @@
     vmem = pl.BlockSpec(memory_space=pltpu.VMEM)
 
     onehots = (west[:, :, None] == jnp.arange(rows, dtype=jnp.int32)).astype(jnp.bfloat16)
-    sigma_tile = jnp.broadcast_to(jnp.pad(sigma, (0, 128 - planes_dev))[None], (8, 128))
     labels, sigma_tiles = pl.pallas_call(
         label_kernel,
         out_shape=(
@@ -571,6 +575,7 @@
         in_specs=[vmem] * 2,
         out_specs=(vmem, vmem),
         scratch_shapes=[
+            pltpu.VMEM((8, 128), jnp.float32),
             pltpu.VMEM((columns, rows, 128), jnp.bfloat16),
             pltpu.VMEM((rows, 128), jnp.bfloat16),
             pltpu.VMEM((strips, rows, 128), jnp.bfloat16),
@@ -580,9 +585,8 @@
             pltpu.SemaphoreType.DMA((shares,)),
         ],
         compiler_params=pltpu.CompilerParams(collective_id=0, has_side_effects=True),
-    )(onehots, sigma_tile)
+    )(onehots, sigma.reshape(1, planes_dev))
     labels = labels[:, :, :rows]
-    sigma_all = sigma_tiles[:, 0, :planes_dev].reshape(planes)
 
     row_ids = jnp.arange(rows, dtype=jnp.int32)
     whole = labels.astype(jnp.int32)
@@ -633,9 +637,9 @@
             pltpu.SemaphoreType.DMA((4,)),
         ],
         compiler_params=pltpu.CompilerParams(
-            vmem_limit_bytes=48 * 1024 * 1024, collective_id=1, has_side_effects=True
+            vmem_limit_bytes=60 * 1024 * 1024, collective_id=1, has_side_effects=True
         ),
-    )(outgoing, sigma_all.reshape(1, planes), matrices, fhi, flo, bhi, blo)
+    )(outgoing, sigma_tiles, matrices, fhi, flo, bhi, blo)
 
     return pl.pallas_call(
         lambda *refs: unpack_kernel(strips, *refs),

time: 123 us -> 122 us (level)
  local copies, waits for them, and re-layouts: 7.35 us -> 3.95 us
  Pallas kernels: 98.9 us -> 101 us
    pallas_call x1, Pallas kernels: 84.3 us -> 86.6 us  [chain_on_device(): pl.pallas_call(lambda *refs: chain_kernel(shares, strips, half_cols, *ref...]
    unnamed x18 -> x12, local copies, waits for them, and re-layouts: 3.83 us -> 3.09 us
  transfers between devices with their start and end apart: 1 -> 1, of which waited for: 1 -> 1; matrix products, arithmetic and copies ran while one was open for 2% -> 0% of each run, Pallas kernels for 2% -> 2%
where the time goes in v5:
time: 122 us; the launch traced here: 121 us
  Pallas kernels  101 us (83%)
  waiting for transfers between devices  7.53 us (6%)
  starting transfers between devices  4.7 us (4%)
  local copies, waits for them, and re-layouts  3.95 us (3%)
  matrix products  1.71 us (1%)
  other arithmetic  1.6 us (1%)
    pallas_call x1, Pallas kernels, chain_on_device(): pl.pallas_call(lambda *refs: chain_kernel(shares, strips, half_cols, *ref...  86.6 us
    pallas_call x1, Pallas kernels, chain_on_device(): pl.pallas_call(label_kernel, out_shape=(jax.ShapeDtypeStruct((columns, ro...  8.76 us
    all_to_all x1, waiting for transfers between devices, chain_on_device(): matrices = lax.all_to_all(matrices, 'strip', 0, 0, tiled=True)  7.53 us
    all_to_all x1, starting transfers between devices, chain_on_device(): matrices = lax.all_to_all(matrices, 'strip', 0, 0, tiled=True)  4.7 us
    pallas_call x1, Pallas kernels, chain_on_device(): pl.pallas_call(lambda *refs: unpack_kernel(strips, *refs), out_shape=(jax...  3.31 us
    unnamed x12, local copies, waits for them, and re-layouts  3.09 us
    pallas_call x1, Pallas kernels, chain_on_device(): pl.pallas_call(lambda *refs: pack_kernel(strips, *refs), out_shape=jax.Sh...  2.53 us
  transfers between devices with their start and end apart: 1, of which 1 were waited for; matrix products, arithmetic and copies ran while one was open for 0% of the time, Pallas kernels for 2%

profile of v5, /device:TPU:5, one launch (start us, length us, event | category | flops | bytes accessed | tf_op | source)
XLA Modules:
  0.0 121.5 jit_solution(9645293547795928746)
XLA Ops:
  0.6 1.4 %fusion.7.onehot_ref = bf16[8,16,16]{2,1,0:T(8,128)(2,1)} fusion(s32[8,16]{1,0:T(8,128)} %param.14), kind=kLoop, calls=%fused_computation.11 | loop fusion | flops 4096 | bytes 4608 | tf_op jit(solution)/shard_map/convert_element_type | solution.py:568
  2.0 8.8 %shard_map.122 = (bf16[8,16,128]{2,1,0:T(8,128)(2,1)}, f32[4,8,128]{2,1,0:T(8,128)}) custom-call(bf16[8,16,16]{2,1,0:T(8,128)(2,1)} %fusion.7.onehot_ref, f32[1,64]{1,0:T(1,128)} %bitcast.15), custom_call_target="tpu_custom_call" | custom-call | tf_op jit(solution)/shard_map/pallas_call | solution.py:569
  10.8 1.7 %convolution_bitcast_fusion = bf16[8,3,8,1296]{3,0,1,2:T(8,128)(2,1)S(1)} fusion(bf16[1,8,16,1296]{3,2,0,1:T(8,128)(2,1)} %bitcast.16, bf16[1,8,16,1296]{3,2,0,1:T(8,128)(2,1)} %bitcast.17, bf16[1,8,16,1296]{3,2,0,1:T(8,128)(2,1)} %bitcast.18, bf16[8,16,16]{2,1,0:T(8,128)(2,1)} %bitcast.14, s32[]{:T(128)S(6)} %select_n.9), kind=kOutput, calls=%fused_computation | convolution fusion | flops 8957952 | bytes 1497092 | tf_op jit(solution)/shard_map/grc,mgre->cmge/dot_general | solution.py:614
  12.5 0.0 copy-start.5
  12.5 0.0 copy-start.2
  12.5 0.0 copy-start.3
  12.6 0.9 copy.19
  13.4 4.7 %all-to-all-start = ((bf16[8,3,8,1296]{3,2,1,0:T(8,128)(2,1)}), bf16[8,3,8,1296]{3,2,1,0:T(8,128)(2,1)S(1)}, u32[]{:S(2)}, u32[]{:S(2)}) async-start(bf16[8,3,8,1296]{3,2,1,0:T(8,128)(2,1)} %copy.19), calls=%async_computation | async-start | bytes 1081344 | tf_op jit(solution)/shard_map/all_to_all | solution.py:615
  18.1 0.0 copy-done.5
  18.1 0.2 fusion.6
  18.3 0.0 copy-done.2
  18.3 0.0 copy-done.3
  18.4 2.5 %shard_map.123.refs_0_ = bf16[32,144,128]{2,1,0:T(8,128)(2,1)S(1)} custom-call(s32[8,16]{1,0:T(8,128)S(1)} %get-tuple-element.6.refs_0_, bf16[64,8,576]{2,1,0:T(8,128)(2,1)S(1)} %copy-done.2, bf16[64,8,576]{2,1,0:T(8,128)(2,1)S(1)} %copy-done.3), custom_call_target="tpu_custom_call" | custom-call | tf_op jit(solution)/shard_map/pallas_call | solution.py:600
  20.9 0.0 copy-start
  20.9 1.0 copy-done
  21.9 7.5 %all-to-all-done = bf16[8,3,8,1296]{3,2,1,0:T(8,128)(2,1)S(1)} async-done(((bf16[8,3,8,1296]{3,2,1,0:T(8,128)(2,1)}), bf16[8,3,8,1296]{3,2,1,0:T(8,128)(2,1)S(1)}, u32[]{:S(2)}, u32[]{:S(2)}) %all-to-all-start) | async-done | bytes 497696 | tf_op jit(solution)/shard_map/all_to_all | solution.py:615
  29.4 0.0 copy-start.4
  29.4 0.8 copy-done.4
  30.2 86.6 %shard_map.124.refs_1_ = bf16[32,144,128]{2,1,0:T(8,128)(2,1)} custom-call(bf16[32,144,128]{2,1,0:T(8,128)(2,1)} %copy-done, f32[4,8,128]{2,1,0:T(8,128)} %get-tuple-element.5.refs_1_, bf16[8,24,1296]{2,1,0:T(8,128)(2,1)} %bitcast.13, bf16[512,512]{1,0:T(8,128)(2,1)} %constant.32.clone.refs_3_, bf16[512,512]{1,0:T(8,128)(2,1)} %constant.33.clone.refs_4_, ...), custom_call_target="tpu_custom_call" | custom-call | tf_op jit(solution)/shard_map/pallas_call | solution.py:619
  116.9 0.0 copy-start.1
  116.9 1.3 %copy-done.1 = bf16[32,144,128]{2,1,0:T(8,128)(2,1)S(1)} copy-done((bf16[32,144,128]{2,1,0:T(8,128)(2,1)S(1)}, bf16[32,144,128]{2,1,0:T(8,128)(2,1)}, u32[]{:S(2)}) %copy-start.1) | copy-done | bytes 1179672
  118.2 3.3 %shard_map.125 = (bf16[64,8,576]{2,1,0:T(8,128)(2,1)}, bf16[64,8,576]{2,1,0:T(8,128)(2,1)}) custom-call(s32[8,16]{1,0:T(8,128)S(1)} %get-tuple-element.7.refs_0_, bf16[32,144,128]{2,1,0:T(8,128)(2,1)S(1)} %copy-done.1), custom_call_target="tpu_custom_call" | custom-call | tf_op jit(solution)/shard_map/pallas_call | solution.py:644
Async XLA Ops:
  12.5 5.6 %copy-start.5 = (bf16[8,16,128]{2,1,0:T(8,128)(2,1)S(1)}, bf16[8,16,128]{2,1,0:T(8,128)(2,1)}, u32[]{:S(2)}) copy-start(bf16[8,16,128]{2,1,0:T(8,128)(2,1)} %get-tuple-element.4) | copy-start | bytes 98308
  12.5 5.8 %copy-start.2 = (bf16[64,8,576]{2,1,0:T(8,128)(2,1)S(1)}, bf16[64,8,576]{2,1,0:T(8,128)(2,1)}, u32[]{:S(2)}) copy-start(bf16[64,8,576]{2,1,0:T(8,128)(2,1)} %refs_1_.1) | copy-start | bytes 1769476
  12.5 5.8 %copy-start.3 = (bf16[64,8,576]{2,1,0:T(8,128)(2,1)S(1)}, bf16[64,8,576]{2,1,0:T(8,128)(2,1)}, u32[]{:S(2)}) copy-start(bf16[64,8,576]{2,1,0:T(8,128)(2,1)} %refs_2_.1) | copy-start | bytes 1769476
  13.4 16.0 %all-to-all-start = ((bf16[8,3,8,1296]{3,2,1,0:T(8,128)(2,1)}), bf16[8,3,8,1296]{3,2,1,0:T(8,128)(2,1)S(1)}, u32[]{:S(2)}, u32[]{:S(2)}) async-start(bf16[8,3,8,1296]{3,2,1,0:T(8,128)(2,1)} %copy.19), calls=%async_computation | async-start | bytes 1081344 | tf_op jit(solution)/shard_map/all_to_all | solution.py:615
  20.9 1.0 copy-start
  29.4 0.8 copy-start.4
  116.9 1.3 %copy-start.1 = (bf16[32,144,128]{2,1,0:T(8,128)(2,1)S(1)}, bf16[32,144,128]{2,1,0:T(8,128)(2,1)}, u32[]{:S(2)}) copy-start(bf16[32,144,128]{2,1,0:T(8,128)(2,1)} %shard_map.124.refs_1_) | copy-start | bytes 3538948
